TPU v7x, 32 devices: a whole 2x2x4 slice. The times are simulated.
32 devices in a mesh: groups: 2 (over y), slab: 4 (over z), chan: 4 (over x, core).
Axes of the slice: x: 2, y: 2, z: 4, core: 2. Of those that a mesh axis runs over, the one named last changes fastest.
Arguments:
- inputs: float32 [256, 128, 20, 128], P(('groups', 'slab'), 'chan'), parts along dimension 0, may hold values from -6 to 6
- cotangent: float32 [256, 128, 20, 128], P(('groups', 'slab'), 'chan'), parts along dimension 0, may hold values from -6 to 6
- spectral: float32 [32, 32, 2, 20, 640], P('slab', 'chan'), may hold values from -2.5 to 2.5
- local_weight: float32 [20, 20], replicated, may hold values from -1.25 to 1.25
- bias_vector: float32 [20], replicated, may hold values from -3 to 3
Outputs:
- output: float32 [256, 128, 20, 128], P(('groups', 'slab'), 'chan'), parts along dimension 0
- grad_inputs: float32 [256, 128, 20, 128], P(('groups', 'slab'), 'chan'), parts along dimension 0
- grad_spectral: float32 [64, 32, 2, 20, 640], P(('groups', 'slab'), 'chan'), parts along dimension 0
There are 2 independent parts, one for each index of `groups`. A program takes and returns all parts, laid end to end along the dimension named above; an argument that names none is the same for every part. Nothing has to cross between parts.
All inputs are finite; a program needn't handle non-finite values.
Results may differ from a plain program's by a relative error of at most 0.0001.
Values sent between devices are 32-bit elements; how exact they have to be, the bound alone decides.
No kernel may reach another device: no remote copies, remote signals or barrier semaphores. Data moves between devices by JAX's collectives and lax.ppermute only.
A program may use at most 320 MiB of HBM per device.

v0:
```python
from functools import partial
import math

import jax
import jax.numpy as jnp
from jax import lax
from jax.sharding import PartitionSpec as P

NX = 128
NY = 128
NZ = 128
C = 20
MX = 32
MY = 32
MZ = 32


highest = lax.Precision.HIGHEST
root_half = 0.7071067811865476
inv_root_two_pi = 0.3989422804014327


def basis(length, kept_count, offset, row_count, direction):
    position = lax.iota(jnp.int32, row_count) + offset
    frequency = lax.iota(jnp.int32, kept_count)
    frequency = frequency - kept_count * (frequency >= kept_count // 2).astype(jnp.int32)
    phase = frequency[:, None] * position[None, :] % length
    angle = phase.astype(jnp.float32) * (2.0 * math.pi / length)
    factor = 1.0 / math.sqrt(length)
    return (jnp.cos(angle) * factor, direction * jnp.sin(angle) * factor)


def complex_block(length, kept_count, offset, row_count, direction):
    real_part, imag_part = basis(length, kept_count, offset, row_count, direction)
    return jnp.stack([jnp.stack([real_part, -imag_part]), jnp.stack([imag_part, real_part])])


def forward_modes(values):
    rows_x, rows_y = (values.shape[0], values.shape[1])
    real_part, imag_part = basis(NZ, MZ, 0, NZ, -1.0)
    depth_table = jnp.stack([real_part, imag_part])
    depth = jnp.einsum("xycz,pkz->kyxpc", values, depth_table, precision=highest)
    col_table = complex_block(NY, MY, lax.axis_index("chan") * rows_y, rows_y, -1.0)
    piece_rows = lax.slice_in_dim(
        depth, 0, lax.axis_size("chan") * (MZ // lax.axis_size("chan")), axis=0
    )
    middle = lax.psum_scatter(
        jnp.einsum("qpbn,knxpc->kbxqc", col_table, piece_rows, precision=highest),
        "chan",
        scatter_dimension=0,
        tiled=True,
    )
    lines = jnp.transpose(middle, (1, 2, 0, 3, 4))
    row_table = complex_block(NX, MX, lax.axis_index("slab") * rows_x, rows_x, -1.0)
    piece_rows = lax.slice_in_dim(
        lines, 0, lax.axis_size("slab") * (MY // lax.axis_size("slab")), axis=0
    )
    return lax.psum_scatter(
        jnp.einsum("qpan,bnkpc->bakqc", row_table, piece_rows, precision=highest),
        "slab",
        scatter_dimension=0,
        tiled=True,
    )


def inverse_field(spectrum):
    second_local, depth_local = (spectrum.shape[0], spectrum.shape[2])
    row_table = complex_block(NX, MX, 0, NX, 1.0)
    columns = jnp.einsum("qpan,bakpc->bnkqc", row_table, spectrum, precision=highest)
    columns = lax.all_to_all(
        columns.reshape(second_local, NX, depth_local * 2 * C),
        "slab",
        split_axis=1,
        concat_axis=0,
        tiled=True,
    )
    rows_x = columns.shape[1]
    columns = columns.reshape(MY, rows_x, depth_local, 2, C)
    col_table = complex_block(NY, MY, 0, NY, 1.0)
    planes = jnp.einsum("qpbn,bxkpc->knxqc", col_table, columns, precision=highest)
    planes = lax.all_to_all(
        planes.reshape(depth_local, NY, rows_x * 2 * C),
        "chan",
        split_axis=1,
        concat_axis=0,
        tiled=True,
    )
    rows_y = planes.shape[1]
    planes = planes.reshape(MZ, rows_y, rows_x, 2, C)
    real_part, imag_part = basis(NZ, MZ, 0, NZ, 1.0)
    depth_table = jnp.stack([real_part, -imag_part])
    return jnp.einsum("pkz,kyxpc->xycz", depth_table, planes, precision=highest)


def smooth_gate(values):
    return 0.5 * values * (1.0 + jax.scipy.special.erf(values * root_half))


def gate_slope(values):
    return (
        0.5 * (1.0 + jax.scipy.special.erf(values * root_half))
        + values * jnp.exp(-0.5 * values * values) * inv_root_two_pi
    )


def local(inputs, cotangent, spectral, local_weight, bias_vector):
    mixer = partial(jnp.einsum, precision=highest)
    second_local, depth_local = (spectral.shape[0], spectral.shape[1])
    weights = spectral.reshape(second_local, depth_local, 2, C, C, MX)
    w_real, w_imag = (weights[:, :, 0], weights[:, :, 1])
    in_modes = forward_modes(inputs)
    x_real, x_imag = (in_modes[:, :, :, 0], in_modes[:, :, :, 1])
    y_real = mixer("bkioa,baki->bako", w_real, x_real) - mixer("bkioa,baki->bako", w_imag, x_imag)
    y_imag = mixer("bkioa,baki->bako", w_real, x_imag) + mixer("bkioa,baki->bako", w_imag, x_real)
    spectral_part = inverse_field(jnp.stack([y_real, y_imag], axis=3))
    linear_sum = spectral_part + mixer("xycz,co->xyoz", inputs, local_weight) + bias_vector[:, None]
    output = smooth_gate(linear_sum)
    pre_gradient = cotangent * gate_slope(linear_sum)
    grad_modes = forward_modes(pre_gradient)
    g_real, g_imag = (grad_modes[:, :, :, 0], grad_modes[:, :, :, 1])
    grad_real = mixer("bako,baki->bkioa", g_real, x_real) + mixer(
        "bako,baki->bkioa", g_imag, x_imag
    )
    grad_imag = mixer("bako,baki->bkioa", g_imag, x_real) - mixer(
        "bako,baki->bkioa", g_real, x_imag
    )
    grad_spectral = jnp.stack([grad_real, grad_imag], axis=2).reshape(
        second_local, depth_local, 2, C, C * MX
    )
    back_real = mixer("bkioa,bako->baki", w_real, g_real) + mixer(
        "bkioa,bako->baki", w_imag, g_imag
    )
    back_imag = mixer("bkioa,bako->baki", w_real, g_imag) - mixer(
        "bkioa,bako->baki", w_imag, g_real
    )
    grad_inputs = inverse_field(jnp.stack([back_real, back_imag], axis=3)) + mixer(
        "xyoz,co->xycz", pre_gradient, local_weight
    )
    return (output, grad_inputs, grad_spectral)


def solution(mesh):
    in_specs = (
        P(("groups", "slab"), "chan", None, None),
        P(("groups", "slab"), "chan", None, None),
        P("slab", "chan", None, None, None),
        P(),
        P(),
    )
    out_specs = (
        P(("groups", "slab"), "chan", None, None),
        P(("groups", "slab"), "chan", None, None),
        P(("groups", "slab"), "chan", None, None, None),
    )
    return jax.shard_map(local, mesh=mesh, in_specs=in_specs, out_specs=out_specs, check_vma=False)
```

profile of v0, /device:TPU:0, one launch (start us, length us, event | category | flops | bytes accessed | tf_op | source)
XLA Modules:
  0.0 1221.4 jit_solution(4761653234677751829)
XLA Ops:
  7.7 53.0 %fusion.33 = f32[32,32,32,2,20,1]{1,0,4,2,3,5:T(8,128)S(1)} fusion(f32[32,32,20,128]{3,1,2,0:T(8,128)} %param.5, f32[1,32,128]{2,1,0:T(8,128)S(1)} %get-tuple-element.57, f32[1,32,128]{2,1,0:T(8,128)S(1)} %get-tuple-element.56), kind=kOutput, calls=%fused_computation.44 | convolution fusion | flops 2013274112 | bytes 15761408 | tf_op jit(solution)/shard_map/xycz,pkz->kyxpc/dot_general | solution.py:42
  60.6 35.5 %fusion.27 = f32[32,32,32,2,20]{1,2,3,4,0:T(8,128)} fusion(f32[32,32,32,2,20,1]{1,0,4,2,3,5:T(8,128)S(1)} %fusion.33, f32[1,2,32,32]{3,2,1,0:T(8,128)S(1)} %get-tuple-element.47, f32[1,2,32,32]{3,2,1,0:T(8,128)S(1)} %get-tuple-element.46), kind=kOutput, calls=%fused_computation.42 | convolution fusion | flops 1006637056 | bytes 10502144 | tf_op jit(solution)/shard_map/qpbn,knxpc->kbxqc/dot_general | solution.py:48
  96.2 155.9 %reduce-scatter.5.cloned.1.call-done = f32[8,32,32,2,20]{1,2,3,4,0:T(8,128)} async-done(((f32[32,32,32,2,20]{1,2,3,4,0:T(8,128)}), f32[8,32,32,2,20]{1,2,3,4,0:T(8,128)}) %reduce-scatter.5.cloned.1.call-update) | async-done | bytes 1310736 | tf_op jit(solution)/shard_map/reduce_scatter | solution.py:47
  252.1 12.0 fusion.43
  271.3 19.8 %reshape.567 = f32[8,8,2,20,20,32]{5,4,1,3,2,0:T(8,128)} reshape(f32[8,8,2,20,640]{4,1,3,2,0:T(8,128)} %copy.124) | data formatting | bytes 13107200 | tf_op jit(solution)/shard_map/reshape | solution.py:109
  291.1 67.0 %reduce-scatter.7.cloned.1.call-done = f32[8,32,8,2,20]{1,0,3,4,2:T(8,128)} async-done(((f32[32,32,8,2,20]{1,0,3,4,2:T(8,128)}), f32[8,32,8,2,20]{1,0,3,4,2:T(8,128)}) %reduce-scatter.7.cloned.1.call-update) | async-done | bytes 327696 | tf_op jit(solution)/shard_map/reduce_scatter | solution.py:58
  361.4 13.5 %fusion.8 = (f32[8,32,8,20]{1,3,2,0:T(8,128)S(1)}, f32[8,32,8,20]{1,3,2,0:T(8,128)S(1)}, f32[8,32,8,20]{1,3,2,0:T(8,128)S(1)}, f32[8,32,8,20]{1,3,2,0:T(8,128)S(1)}) fusion(f32[8,8,2,20,20,32]{5,4,1,3,2,0:T(8,128)} %reshape.567, f32[8,32,8,20]{1,2,3,0:T(8,128)S(1)} %copy.256, f32[8,32,8,20]{1,2,3,0:T(8,128)S(1)} %copy.255), kind=kLoop, calls=%fused_computation.14 | loop fusion | flops 6389760 | bytes 7536640 | tf_op jit(solution)/shard_map/bkioa,baki->bako/dot_general | solution.py:113
  378.0 41.0 %all_to_all.60 = f32[8,128,320]{2,0,1:T(8,128)S(1)} all-to-all(f32[8,128,320]{2,0,1:T(8,128)S(1)} %copy.126), channel_id=1, replica_groups=mesh['groups'=2,'slab'=4,'chan'=4] {'slab'}, dimensions={1} | all-to-all | bytes 2621440 | tf_op jit(solution)/shard_map/all_to_all | solution.py:70
  451.6 21.4 %fusion.14 = f32[20,32,32,128]{3,0,2,1:T(8,128)} fusion(f32[32,32,20,128]{3,1,2,0:T(8,128)} %param.5, f32[20,20]{1,0:T(8,128)S(1)} %copy-done), kind=kOutput, calls=%fused_computation.25 | convolution fusion | flops 629145600 | bytes 20973120 | tf_op jit(solution)/shard_map/xycz,co->xyoz/dot_general | solution.py:116
  473.0 38.1 %all-to-all-done.1 = f32[8,128,1280]{2,0,1:T(8,128)} async-done(((f32[8,128,1280]{2,0,1:T(8,128)}), f32[8,128,1280]{2,0,1:T(8,128)}, u32[]{:S(2)}, u32[]{:S(2)}) %all-to-all-start.1) | async-done | bytes 5242912 | tf_op jit(solution)/shard_map/all_to_all | solution.py:81
  511.0 17.6 %copy.133 = f32[4,8,32,1280]{2,1,0,3:T(8,128)} copy(f32[4,8,32,1280]{3,1,2,0:T(8,128)} %bitcast.60) | data formatting | bytes 10485760 | tf_op jit(solution)/shard_map/all_to_all | solution.py:81
  528.6 23.6 %copy.134 = f32[32,32,32,2,20]{0,2,3,4,1:T(8,128)} copy(f32[32,32,32,2,20]{1,0,4,3,2:T(8,128)} %bitcast.273) | data formatting | bytes 10485760 | tf_op jit(solution)/shard_map/reshape | solution.py:89
  552.3 40.8 %fusion.20 = (f32[32,32,20,128]{3,0,2,1:T(8,128)S(1)}, f32[32,32,20,128]{3,0,2,1:T(8,128)}) fusion(f32[32,32,20,128]{3,1,2,0:T(8,128)} %param.6, f32[20]{0:T(128)S(1)} %copy-done.6, f32[20,32,32,128]{3,0,2,1:T(8,128)} %fusion.14, f32[32,32,32,2,20]{0,2,3,4,1:T(8,128)} %copy.134, f32[1,32,128]{2,1,0:T(8,128)S(1)} %get-tuple-element.54, ...), kind=kOutput, calls=%fused_computation.31 | convolution fusion | flops 2047352832 | bytes 47218768 | tf_op jit(solution)/shard_map/pkz,kyxpc->xycz/dot_general | solution.py:92
  593.0 58.6 %fusion.36 = f32[32,32,32,2,20,1]{1,0,4,2,3,5:T(8,128)} fusion(f32[32,32,20,128]{3,0,2,1:T(8,128)S(1)} %get-tuple-element.30, f32[1,32,128]{2,1,0:T(8,128)S(1)} %get-tuple-element.57, f32[1,32,128]{2,1,0:T(8,128)S(1)} %get-tuple-element.56), kind=kOutput, calls=%fused_computation.45 | convolution fusion | flops 2013274112 | bytes 15761408 | tf_op jit(solution)/shard_map/xycz,pkz->kyxpc/dot_general | solution.py:42
  651.7 38.4 %fusion.30 = f32[32,32,32,2,20]{1,2,3,4,0:T(8,128)} fusion(f32[32,32,32,2,20,1]{1,0,4,2,3,5:T(8,128)} %fusion.36, f32[1,2,32,32]{3,2,1,0:T(8,128)S(1)} %get-tuple-element.47, f32[1,2,32,32]{3,2,1,0:T(8,128)S(1)} %get-tuple-element.46), kind=kOutput, calls=%fused_computation.43 | convolution fusion | flops 1006637056 | bytes 10502144 | tf_op jit(solution)/shard_map/qpbn,knxpc->kbxqc/dot_general | solution.py:48
  690.1 151.4 %reduce-scatter.9.cloned.1.call-done = f32[8,32,32,2,20]{1,2,3,4,0:T(8,128)} async-done(((f32[32,32,32,2,20]{1,2,3,4,0:T(8,128)}), f32[8,32,32,2,20]{1,2,3,4,0:T(8,128)}) %reduce-scatter.9.cloned.1.call-update) | async-done | bytes 1310736 | tf_op jit(solution)/shard_map/reduce_scatter | solution.py:47
  853.4 93.9 %reduce-scatter.11.cloned.1.call-done = f32[8,32,8,2,20]{1,0,3,4,2:T(8,128)} async-done(((f32[32,32,8,2,20]{1,0,3,4,2:T(8,128)}), f32[8,32,8,2,20]{1,0,3,4,2:T(8,128)}) %reduce-scatter.11.cloned.1.call-update) | async-done | bytes 327696 | tf_op jit(solution)/shard_map/reduce_scatter | solution.py:58
  950.2 17.9 %fusion.6 = (f32[8,32,8,20]{1,2,3,0:T(8,128)S(1)}, f32[8,32,8,20]{1,2,3,0:T(8,128)S(1)}, f32[8,32,8,20]{1,2,3,0:T(8,128)S(1)}, f32[8,32,8,20]{1,2,3,0:T(8,128)S(1)}) fusion(f32[8,8,2,20,20,32]{5,4,1,3,2,0:T(8,128)} %reshape.567, f32[8,32,8,20]{1,3,2,0:T(8,128)S(1)} %copy.257, f32[8,32,8,20]{1,3,2,0:T(8,128)S(1)} %copy.258), kind=kLoop, calls=%fused_computation.10 | loop fusion | flops 6389760 | bytes 7536640
  971.4 41.4 %all_to_all.61 = f32[8,128,320]{2,0,1:T(8,128)S(1)} all-to-all(f32[8,128,320]{2,0,1:T(8,128)S(1)} %copy.143), channel_id=1, replica_groups=mesh['groups'=2,'slab'=4,'chan'=4] {'slab'}, dimensions={1} | all-to-all | bytes 2621440 | tf_op jit(solution)/shard_map/all_to_all | solution.py:70
  1046.4 14.3 %copy.158 = f32[32,32,20,128]{3,1,2,0:T(8,128)} copy(f32[32,32,20,128]{3,0,2,1:T(8,128)} %get-tuple-element.31) | data formatting | bytes 20971520
  1060.7 26.1 %fusion.12 = f32[32,32,128,20]{2,3,1,0:T(8,128)} fusion(f32[32,32,20,128]{3,0,2,1:T(8,128)S(1)} %bitcast.272, f32[20,20]{1,0:T(8,128)S(1)} %copy-done), kind=kOutput, calls=%fused_computation.23 | convolution fusion | flops 629145600 | bytes 20973120 | tf_op jit(solution)/shard_map/xyoz,co->xycz/dot_general | solution.py:136
  1136.0 17.5 %copy.150 = f32[4,8,32,1280]{2,1,0,3:T(8,128)} copy(f32[4,8,32,1280]{3,1,2,0:T(8,128)} %bitcast.109) | data formatting | bytes 10485760 | tf_op jit(solution)/shard_map/all_to_all | solution.py:81
  1153.5 23.6 %copy.151 = f32[32,32,32,2,20]{0,2,3,4,1:T(8,128)} copy(f32[32,32,32,2,20]{1,0,4,3,2:T(8,128)} %bitcast.274) | data formatting | bytes 10485760 | tf_op jit(solution)/shard_map/reshape | solution.py:89
  1177.1 27.1 %bitcast_add_fusion = f32[32,32,20,128]{3,0,2,1:T(8,128)S(1)} fusion(f32[32,32,128,20]{2,3,1,0:T(8,128)} %fusion.12, f32[32,32,32,2,20]{0,2,3,4,1:T(8,128)} %copy.151, f32[1,32,128]{2,1,0:T(8,128)S(1)} %get-tuple-element.57, f32[1,32,128]{2,1,0:T(8,128)S(1)} %get-tuple-element.54), kind=kOutput, calls=%fused_computation.32 | convolution fusion | flops 2015895552 | bytes 26247168 | tf_op jit(solution)/shard_map/pkz,kyxpc->xycz/dot_general | solution.py:92
  (77 shorter events, 157.6 us)
Async XLA Ops:
  7.2 444.5 %copy-start = (f32[20,20]{1,0:T(8,128)S(1)}, f32[20,20]{1,0:T(8,128)}, u32[]{:S(2)}) copy-start(f32[20,20]{1,0:T(8,128)} %param.8) | copy-start | bytes 4804
  7.2 245.0 %reduce-scatter.5.cloned.1.call-start = ((), (), s32[]{:S(2)}) async-start(), calls=%async_computation.8 | async-start | bytes 26214400 | tf_op jit(solution)/shard_map/reduce_scatter | solution.py:47
  96.2 261.9 %reduce-scatter.7.cloned.1.call-start = ((), (), s32[]{:S(2)}) async-start(), calls=%async_computation.9 | async-start | bytes 6553600 | tf_op jit(solution)/shard_map/reduce_scatter | solution.py:58
  446.5 64.5 %all-to-all-start.1 = ((f32[8,128,1280]{2,0,1:T(8,128)}), f32[8,128,1280]{2,0,1:T(8,128)}, u32[]{:S(2)}, u32[]{:S(2)}) async-start(f32[8,128,1280]{2,0,1:T(8,128)} %copy.131), calls=%async_computation.3 | async-start | bytes 10485760 | tf_op jit(solution)/shard_map/all_to_all | solution.py:81
  451.6 389.9 %reduce-scatter.9.cloned.1.call-start = ((), (), s32[]{:S(2)}) async-start(), calls=%async_computation.10 | async-start | bytes 26214400 | tf_op jit(solution)/shard_map/reduce_scatter | solution.py:47
  528.6 23.6 %copy-start.6 = (f32[20]{0:T(128)S(1)}, f32[20]{0:T(128)}, u32[]{:S(2)}) copy-start(f32[20]{0:T(128)} %param.9) | copy-start | bytes 244
  593.0 58.6 %copy-start.1 = (f32[32,32,20,128]{3,0,2,1:T(8,128)}, f32[32,32,20,128]{3,0,2,1:T(8,128)S(1)}, u32[]{:S(2)}) copy-start(f32[32,32,20,128]{3,0,2,1:T(8,128)S(1)} %get-tuple-element.30) | copy-start | bytes 31457284
  690.1 257.3 %reduce-scatter.11.cloned.1.call-start = ((), (), s32[]{:S(2)}) async-start(), calls=%async_computation.11 | async-start | bytes 6553600 | tf_op jit(solution)/shard_map/reduce_scatter | solution.py:58
  1034.1 11.5 copy-start.3
  1034.1 11.9 copy-start.2
  1040.5 95.5 %all-to-all-start.3 = ((f32[8,128,1280]{2,0,1:T(8,128)}), f32[8,128,1280]{2,0,1:T(8,128)}, u32[]{:S(2)}, u32[]{:S(2)}) async-start(f32[8,128,1280]{2,0,1:T(8,128)} %copy.148), calls=%async_computation.7 | async-start | bytes 10485760 | tf_op jit(solution)/shard_map/all_to_all | solution.py:81
  1046.4 14.3 %slice-start = ((s8[10485760]{0:T(1024)(128)(4,1)}), s8[4194304]{0:T(1024)(128)(4,1)S(1)}, s32[]{:S(2)}) async-start(s8[10485760]{0:T(1024)(128)(4,1)} %bitcast.271), calls=%async_computation.12 | async-start | bytes 8388608
  1046.4 14.3 %slice-start.1 = ((s8[10485760]{0:T(1024)(128)(4,1)}), s8[4194304]{0:T(1024)(128)(4,1)S(1)}, s32[]{:S(2)}) async-start(s8[10485760]{0:T(1024)(128)(4,1)} %bitcast.271), calls=%async_computation.13 | async-start | bytes 8388608
  1046.4 14.3 %slice-start.2 = ((s8[10485760]{0:T(1024)(128)(4,1)}), s8[2097152]{0:T(1024)(128)(4,1)S(1)}, s32[]{:S(2)}) async-start(s8[10485760]{0:T(1024)(128)(4,1)} %bitcast.271), calls=%async_computation.14 | async-start | bytes 4194304
  1060.7 26.1 %copy-start.5 = (f32[8,8,32,20]{2,0,3,1:T(8,128)S(1)}, f32[8,8,32,20]{2,0,3,1:T(8,128)}, u32[]{:S(2)}) copy-start(f32[8,8,32,20]{2,0,3,1:T(8,128)} %get-tuple-element.38) | copy-start | bytes 491524
  1060.7 26.2 %copy-start.4 = (f32[8,8,32,20]{2,0,3,1:T(8,128)S(1)}, f32[8,8,32,20]{2,0,3,1:T(8,128)}, u32[]{:S(2)}) copy-start(f32[8,8,32,20]{2,0,3,1:T(8,128)} %get-tuple-element.39) | copy-start | bytes 491524
Sparse Core Ops, SparseCore 0:
  96.3 155.8 reduce-scatter.4
  264.2 93.7 reduce-scatter.6
  690.2 151.2 reduce-scatter.8
  853.5 93.7 reduce-scatter.10
where the time goes:
time: 1230 us; the launch traced here: 1220 us
  waiting for transfers between devices  506 us (41%)
  matrix products  340 us (28%)
  local copies, waits for them, and re-layouts  218 us (18%)
  blocking collectives  82.4 us (7%)
  other arithmetic  49.7 us (4%)
  between operations  14.6 us (1%)
    reduce_scatter x2, waiting for transfers between devices, forward_modes(): lax.psum_scatter(jnp.einsum('qpbn,knxpc->kbxqc', col_table, piece_rows, p...  307 us
    reduce_scatter x2, waiting for transfers between devices, forward_modes(): lax.psum_scatter(jnp.einsum('qpan,bnkpc->bakqc', row_table, piece_rows, p...  161 us
    dot_general x2, matrix products, forward_modes(): jnp.einsum('xycz,pkz->kyxpc', values, depth_table, precision=highest)  112 us
    all_to_all x2, blocking collectives, inverse_field(): lax.all_to_all(columns.reshape(second_local, NX, depth_local * 2 * C), 's...  82.4 us
    dot_general x2, matrix products, forward_modes(): jnp.einsum('qpbn,knxpc->kbxqc', col_table, piece_rows, precision=highest)  73.9 us
    dot_general x2, matrix products, inverse_field(): return jnp.einsum('pkz,kyxpc->xycz', depth_table, planes, precision=highest)  67.9 us
    reshape x2, local copies, waits for them, and re-layouts, inverse_field(): planes = planes.reshape(MZ, rows_y, rows_x, 2, C)  47.3 us
    unnamed x28, local copies, waits for them, and re-layouts  43.4 us
  transfers between devices with their start and end apart: 6, of which 5 were waited for; matrix products, arithmetic and copies ran while one was open for 11% of the time, Pallas kernels for 0%

commit v1 on v0

v1 whole, which is shorter than its diff:
```python
from functools import partial
import math

import jax
import jax.numpy as jnp
import ml_dtypes
import numpy as np
from jax import lax
from jax.experimental import pallas as pl
from jax.experimental.pallas import tpu as pltpu
from jax.sharding import PartitionSpec as P

f32 = jnp.float32
bf16 = jnp.bfloat16
root_half = 0.7071067811865476
inv_root_two_pi = 0.3989422804014327
VMEM_LIMIT = 60 * 1024 * 1024
NT = (((1,), (1,)), ((), ()))
TN = (((0,), (0,)), ((), ()))


def round_up(value, unit):
    return -(-value // unit) * unit


class Plan:
    def __init__(self, nx, ny, nz, channels, wb, wk, mx, slab_count, chan_count):
        self.nx, self.ny, self.nz, self.c = nx, ny, nz, channels
        self.wb, self.wk, self.mx = wb, wk, mx
        self.s, self.ch = slab_count, chan_count
        self.half = chan_count // 2
        self.na = mx // 2 + 1
        self.span = (wb + 1) * self.na
        self.lw = slab_count * self.span
        self.lp = round_up(self.lw, 128)
        self.ll = round_up(2 * self.span, 128)
        self.mk = self.half * wk
        self.rc = round_up(2 * self.mk + 2 * self.half, 8)
        self.rt = round_up(channels * (wk + 1), 8)
        self.xb = math.gcd(8, nx)
        self.blk = self.xb * ny
        self.rows = channels * wk
        self.full_x, self.full_y = nx * slab_count, ny * chan_count

    def starts(self):
        kept = self.wb * self.s
        return [g * self.wb - (kept if 2 * g >= self.s else 0) for g in range(self.s)]

    def columns(self):
        b = np.concatenate([np.repeat(np.arange(st, st + self.wb + 1), self.na) for st in self.starts()])
        a = np.tile(np.arange(self.na), self.s * (self.wb + 1))
        return a, b

    def plane_table(self):
        a, b = self.columns()
        x = np.repeat(np.arange(self.nx), self.ny)[:, None]
        y = np.tile(np.arange(self.ny), self.nx)[:, None]
        total = self.full_x * self.full_y
        phase = (a * x * self.full_y + b * y * self.full_x) % total * (2.0 * np.pi / total)
        table = np.zeros((self.nx * self.ny, 2 * self.lp))
        scale = 1.0 / math.sqrt(total)
        table[:, : self.lw] = np.cos(phase) * scale
        table[:, self.lp : self.lp + self.lw] = -np.sin(phase) * scale
        return halves(table)

    def turns(self):
        a, b = self.columns()
        x = (np.arange(self.s) * self.nx)[:, None, None]
        y = (np.arange(self.ch) * self.ny)[None, :, None]
        total = self.full_x * self.full_y
        phase = (a * x * self.full_y + b * y * self.full_x) % total * (2.0 * np.pi / total)
        table = np.zeros((self.s, self.ch, 2, self.lp), np.float32)
        table[:, :, 0, : self.lw] = np.cos(phase)
        table[:, :, 1, : self.lw] = np.sin(phase)
        return table

    def depth_rows(self):
        main = np.arange(self.mk)
        edge = (np.arange(self.half) + 1) * self.wk
        z = np.arange(self.nz)
        scale = 1.0 / math.sqrt(self.nz)
        angle = lambda k: (k[:, None] * z) % self.nz * (2.0 * np.pi / self.nz)
        rows = [np.cos(angle(main)), np.sin(angle(main)), np.cos(angle(edge)), np.sin(angle(edge))]
        table = np.zeros((self.rc, self.nz))
        table[: 2 * self.mk + 2 * self.half] = np.concatenate(rows) * scale
        return halves(table)

    def depth_forward(self):
        high, low = self.depth_rows()
        return np.concatenate(
            [np.concatenate([high, high], 1), np.concatenate([low, np.zeros_like(low)], 1)], 0
        )

    def depth_inverse(self):
        high, low = self.depth_rows()
        table = np.zeros((round_up(3 * self.rc, 16), self.nz), ml_dtypes.bfloat16)
        table[: 3 * self.rc] = np.concatenate([high, high, low], 0)
        return table

    def selections(self):
        quarters = 128 // self.mx
        own = np.zeros((self.wb, 2, self.ll, 2, quarters, self.mx), np.float32)
        for b in range(self.wb):
            for r in range(2):
                for a in range(self.mx):
                    if a < self.mx // 2:
                        own[b, 0, r * self.span + b * self.na + a, r, :, a] = 1.0
                    else:
                        spot = r * self.span + (self.wb - b) * self.na + self.mx - a
                        own[b, 1, spot, r, :, a] = 1.0 - 2.0 * r
        own = own.reshape(self.wb, 2 * self.ll, 256)
        back = np.swapaxes(own, 1, 2)
        return own.astype(ml_dtypes.bfloat16), np.ascontiguousarray(back).astype(ml_dtypes.bfloat16)

    def orders(self):
        table = np.zeros((2, self.rows, self.rt), np.float32)
        for c in range(self.c):
            for k in range(self.wk):
                table[0, c * self.wk + k, c * self.wk + k] = 1.0
                mirrored = self.wk - k
                spot = self.rows + c if mirrored == self.wk else c * self.wk + mirrored
                table[1, c * self.wk + k, spot] = 1.0
        return table.astype(ml_dtypes.bfloat16)


def halves(table):
    high = table.astype(np.float32).astype(ml_dtypes.bfloat16)
    low = (table - high.astype(np.float64)).astype(np.float32).astype(ml_dtypes.bfloat16)
    return high, low


def dot(left, right, numbers=(((1,), (0,)), ((), ()))):
    return lax.dot_general(left, right, numbers, preferred_element_type=f32)


def split(value):
    high = value.astype(bf16)
    return high, (value - high.astype(f32)).astype(bf16)


def moved(value, chosen, left=False):
    first = value.astype(bf16)
    rest = value - first.astype(f32)
    second = rest.astype(bf16)
    third = (rest - second.astype(f32)).astype(bf16)
    if left:
        return dot(chosen, first) + dot(chosen, second) + dot(chosen, third)
    return dot(first, chosen) + dot(second, chosen) + dot(third, chosen)


def depth_analysis(plan, table_ref, values):
    high, low = split(values)
    both = dot(table_ref[...], jnp.concatenate([high, low], axis=1), NT)
    return both[: plan.rc] + both[plan.rc :]


def depth_synthesis(plan, table_ref, rows):
    high = rows.astype(bf16).astype(f32)
    parts = [high, rows - high, high]
    extra = table_ref.shape[0] - 3 * plan.rc
    if extra:
        parts.append(jnp.zeros((extra, rows.shape[1]), f32))
    return dot(jnp.concatenate(parts, axis=0).astype(bf16), table_ref[...], TN)


def plane_analysis(plan, step, lines_ref, high_ref, low_ref, total_ref):
    high, low = split(lines_ref[...].reshape(plan.c * plan.rc, plan.blk))
    for start in range(0, 2 * plan.lp, 256):
        size = min(256, 2 * plan.lp - start)
        columns = pl.ds(start, size)
        part = dot(high, high_ref[:, columns]) + dot(low, high_ref[:, columns]) + dot(high, low_ref[:, columns])
        part = part.reshape(plan.c, plan.rc, size)

        @pl.when(step == 0)
        def _():
            total_ref[:, :, columns] = part

        @pl.when(step > 0)
        def _():
            total_ref[:, :, columns] += part


def plane_synthesis(plan, high_rows, low_rows, high_ref, low_ref, lines_ref):
    high_table, low_table = high_ref[...], low_ref[...]
    lines = (
        dot(high_rows[...], high_table, NT)
        + dot(low_rows[...], high_table, NT)
        + dot(high_rows[...], low_table, NT)
    )
    lines_ref[...] = lines.reshape(plan.c, plan.rc, plan.blk)


def emit_modes(plan, flag_ref, turn_ref, total_ref, keep_ref, send_ref):
    lp, wk, mk, half = plan.lp, plan.wk, plan.mk, plan.half
    odd = flag_ref[0] == 1
    cosine, sine = turn_ref[0:1, :], turn_ref[1:2, :]
    for c in range(plan.c):
        real, imag = total_ref[c, :, :lp], total_ref[c, :, lp:]
        real, imag = real * cosine + imag * sine, imag * cosine - real * sine
        for first, size, base, shift in ((0, wk, c * wk, mk), (2 * mk, 1, plan.rows + c, half)):
            made = []
            for g in range(plan.ch):
                h = g if g < half else plan.ch - 1 - g
                even_rows = slice(first + h * size, first + (h + 1) * size)
                odd_rows = slice(first + shift + h * size, first + shift + (h + 1) * size)
                if g < half:
                    made.append((real[even_rows] + imag[odd_rows], imag[even_rows] - real[odd_rows]))
                else:
                    made.append((real[even_rows] - imag[odd_rows], imag[even_rows] + real[odd_rows]))
            for pair in range(half):
                for r in range(2):
                    low, high = made[2 * pair][r], made[2 * pair + 1][r]
                    keep_ref[pair, r, base : base + size, :] = jnp.where(odd, high, low)
                    send_ref[pair, r, base : base + size, :] = jnp.where(odd, low, high)
    used = plan.c * (wk + 1)
    if used < plan.rt:
        blank = jnp.zeros((plan.half, 2, plan.rt - used, lp), f32)
        keep_ref[:, :, used:, :] = blank
        send_ref[:, :, used:, :] = blank


def take_modes(plan, flag_ref, turn_ref, own_ref, other_ref, total_ref, high_rows, low_rows):
    lp, wk, mk, half = plan.lp, plan.wk, plan.mk, plan.half
    odd = flag_ref[0] == 1
    cosine, sine = turn_ref[0:1, :], turn_ref[1:2, :]

    def group(g, r, rows):
        own, other = own_ref[g // 2, r, rows, :], other_ref[g // 2, r, rows, :]
        return jnp.where(odd, own, other) if g % 2 else jnp.where(odd, other, own)

    for c in range(plan.c):
        for first, size, base, shift in ((0, wk, c * wk, mk), (2 * mk, 1, plan.rows + c, half)):
            rows = slice(base, base + size)
            for h in range(half):
                plus = [group(h, r, rows) for r in range(2)]
                minus = [group(plan.ch - 1 - h, r, rows) for r in range(2)]
                real, imag = plus[0] + minus[0], plus[1] + minus[1]
                here = slice(first + h * size, first + (h + 1) * size)
                total_ref[c, here, :lp] = real * cosine - imag * sine
                total_ref[c, here, lp:] = imag * cosine + real * sine
                real, imag = plus[0] - minus[0], plus[1] - minus[1]
                here = slice(first + shift + h * size, first + shift + (h + 1) * size)
                total_ref[c, here, :lp] = -(imag * cosine + real * sine)
                total_ref[c, here, lp:] = real * cosine - imag * sine
        used = 2 * mk + 2 * half
        if used < plan.rc:
            total_ref[c, used:, :] = jnp.zeros((plan.rc - used, 2 * lp), f32)
    high, low = split(total_ref[...].reshape(plan.c * plan.rc, 2 * lp))
    high_rows[...] = high
    low_rows[...] = low


def analyse_kernel(plan, flag_ref, values_ref, high_ref, low_ref, depth_ref, turn_ref, keep_ref, send_ref, lines_ref, total_ref):
    step = pl.program_id(0)

    @pl.loop(0, plan.c)
    def _(c):
        lines_ref[c] = depth_analysis(plan, depth_ref, values_ref[:, c].reshape(plan.blk, plan.nz))

    plane_analysis(plan, step, lines_ref, high_ref, low_ref, total_ref)

    @pl.when(step == pl.num_programs(0) - 1)
    def _():
        emit_modes(plan, flag_ref, turn_ref, total_ref, keep_ref, send_ref)


def middle_kernel(
    plan, flag_ref, own_ref, other_ref, linear_ref, cotangent_ref, high_ref, low_ref, depth_ref, inverse_ref, turn_ref,
    output_ref, gradient_ref, keep_ref, send_ref, lines_ref, back_ref, total_ref, high_rows, low_rows,
):
    step = pl.program_id(0)

    @pl.when(step == 0)
    def _():
        take_modes(plan, flag_ref, turn_ref, own_ref, other_ref, total_ref, high_rows, low_rows)

    plane_synthesis(plan, high_rows, low_rows, high_ref, low_ref, lines_ref)
    shape = (plan.xb, plan.ny, plan.nz)

    @pl.loop(0, plan.c)
    def _(o):
        field = depth_synthesis(plan, inverse_ref, lines_ref[o])
        value = field + linear_ref[:, o].reshape(plan.blk, plan.nz)
        gate = 0.5 * (1.0 + lax.erf(value * root_half))
        slope = gate + value * jnp.exp(-0.5 * value * value) * inv_root_two_pi
        output_ref[:, o] = (value * gate).reshape(shape)
        gradient = cotangent_ref[:, o].reshape(plan.blk, plan.nz) * slope
        gradient_ref[:, o] = gradient.reshape(shape)
        back_ref[o] = depth_analysis(plan, depth_ref, gradient)

    plane_analysis(plan, step, back_ref, high_ref, low_ref, total_ref)

    @pl.when(step == pl.num_programs(0) - 1)
    def _():
        emit_modes(plan, flag_ref, turn_ref, total_ref, keep_ref, send_ref)


def synthesise_kernel(
    plan, flag_ref, own_ref, other_ref, linear_ref, high_ref, low_ref, inverse_ref, turn_ref,
    output_ref, lines_ref, total_ref, high_rows, low_rows,
):
    @pl.when(pl.program_id(0) == 0)
    def _():
        take_modes(plan, flag_ref, turn_ref, own_ref, other_ref, total_ref, high_rows, low_rows)

    plane_synthesis(plan, high_rows, low_rows, high_ref, low_ref, lines_ref)

    @pl.loop(0, plan.c)
    def _(o):
        value = depth_synthesis(plan, inverse_ref, lines_ref[o]) + linear_ref[:, o].reshape(plan.blk, plan.nz)
        output_ref[:, o] = value.reshape(plan.xb, plan.ny, plan.nz)


def linear_kernel(plan, values_ref, matrix_ref, bias_ref, output_ref):
    tiles = plan.ny // 8
    values = [values_ref[0, :, t * 8 : (t + 1) * 8, :].reshape(plan.c * 8, plan.nz) for t in range(tiles)]
    high, low = split(jnp.concatenate(values, axis=1))
    high_matrix, low_matrix = split(matrix_ref[...])
    mixed = dot(high_matrix, high) + dot(high_matrix, low) + dot(low_matrix, high) + bias_ref[...]
    for t in range(tiles):
        output_ref[0, :, t * 8 : (t + 1) * 8, :] = mixed[:, t * plan.nz : (t + 1) * plan.nz].reshape(plan.c, 8, plan.nz)


def pick(plan, own_ref, mirror_ref, order_ref, chosen_ref, ordered_ref):
    @pl.when(pl.program_id(0) == 0)
    def _():
        ordered_ref[:, : plan.ll] = moved(own_ref[...], order_ref[...], left=True)
        ordered_ref[:, plan.ll :] = moved(mirror_ref[...], order_ref[...], left=True)

    return moved(ordered_ref[...], chosen_ref[0])


def give(plan, made_ref, order_ref, back_ref, own_ref, mirror_ref, sums_ref):
    part = moved(made_ref[...], back_ref[0])
    step = pl.program_id(0)

    @pl.when(step == 0)
    def _():
        sums_ref[...] = part

    @pl.when(step > 0)
    def _():
        sums_ref[...] += part

    @pl.when(step == pl.num_programs(0) - 1)
    def _():
        own_ref[...] = moved(sums_ref[:, : plan.ll], order_ref[...], left=True)
        mirror_ref[...] = moved(sums_ref[:, plan.ll :], order_ref[...], left=True)


def mix_kernel(
    plan, own_ref, mirror_ref, order_ref, disorder_ref, chosen_ref, back_ref, weight_ref,
    modes_ref, own_out, mirror_out, ordered_ref, made_ref, sums_ref,
):
    wk, quarters = plan.wk, 128 // plan.mx
    modes = pick(plan, own_ref, mirror_ref, order_ref, chosen_ref, ordered_ref)
    modes_ref[0] = modes
    place = lax.broadcasted_iota(jnp.int32, (wk, 128), 1) // plan.mx
    for t in range(plan.c // quarters):
        columns = slice(t * 128, (t + 1) * 128)
        real = imag = 0.0
        for i in range(plan.c):
            x_real, x_imag = modes[i * wk : (i + 1) * wk, :128], modes[i * wk : (i + 1) * wk, 128:]
            w_real, w_imag = weight_ref[0, 0, i, :, columns], weight_ref[0, 1, i, :, columns]
            real = real + (w_real * x_real - w_imag * x_imag)
            imag = imag + (w_real * x_imag + w_imag * x_real)
        for q in range(quarters):
            o = t * quarters + q
            made_ref[o * wk : (o + 1) * wk, :128] = jnp.where(place == q, real, 0.0)
            made_ref[o * wk : (o + 1) * wk, 128:] = jnp.where(place == q, imag, 0.0)
    give(plan, made_ref, disorder_ref, back_ref, own_out, mirror_out, sums_ref)


def mix_back_kernel(
    plan, own_ref, mirror_ref, order_ref, disorder_ref, chosen_ref, back_ref, weight_ref, modes_ref,
    gradient_ref, own_out, mirror_out, ordered_ref, made_ref, sums_ref,
):
    wk, quarters = plan.wk, 128 // plan.mx
    grads = pick(plan, own_ref, mirror_ref, order_ref, chosen_ref, ordered_ref)
    place = lax.broadcasted_iota(jnp.int32, (wk, 128), 1) // plan.mx
    lined = []
    for t in range(plan.c // quarters):
        real = imag = 0.0
        for q in range(quarters):
            o = t * quarters + q
            real = jnp.where(place == q, grads[o * wk : (o + 1) * wk, :128], real)
            imag = jnp.where(place == q, grads[o * wk : (o + 1) * wk, 128:], imag)
        lined.append((real, imag))
    for i in range(plan.c):
        rows = slice(i * wk, (i + 1) * wk)
        x_real, x_imag = modes_ref[0, rows, :128], modes_ref[0, rows, 128:]
        back_real = back_imag = 0.0
        for t, (real, imag) in enumerate(lined):
            columns = slice(t * 128, (t + 1) * 128)
            gradient_ref[0, 0, i, :, columns] = real * x_real + imag * x_imag
            gradient_ref[0, 1, i, :, columns] = imag * x_real - real * x_imag
            w_real, w_imag = weight_ref[0, 0, i, :, columns], weight_ref[0, 1, i, :, columns]
            back_real = back_real + (w_real * real + w_imag * imag)
            back_imag = back_imag + (w_real * imag - w_imag * real)
        made_ref[rows, :128] = back_real
        made_ref[rows, 128:] = back_imag
    give(plan, made_ref, disorder_ref, back_ref, own_out, mirror_out, sums_ref)


def whole(array):
    zeros = (0,) * array.ndim
    return pl.BlockSpec(array.shape, lambda i: zeros, pipeline_mode=pl.Buffered(1))


def whole_shape(shape):
    zeros = (0,) * len(shape)
    return pl.BlockSpec(shape, lambda i: zeros, pipeline_mode=pl.Buffered(1))


def leading(shape):
    rest = (0,) * (len(shape) - 1)
    return pl.BlockSpec(shape, lambda i: (i,) + rest)


def shaped(*shape):
    return jax.ShapeDtypeStruct(shape, f32)


def scalar():
    return pl.BlockSpec(memory_space=pltpu.SMEM)


def call(kernel, name, grid, in_specs, out_specs, out_shape, scratch, flops, size):
    return pl.pallas_call(
        kernel,
        grid=(grid,),
        in_specs=in_specs,
        out_specs=out_specs,
        out_shape=out_shape,
        scratch_shapes=scratch,
        name=name,
        compiler_params=pltpu.CompilerParams(vmem_limit_bytes=VMEM_LIMIT, dimension_semantics=("arbitrary",)),
        cost_estimate=pl.CostEstimate(flops=flops, bytes_accessed=size, transcendentals=0),
    )


class Program:
    def __init__(self, plan):
        self.plan = plan
        self.plane = [jnp.asarray(t) for t in plan.plane_table()]
        self.depth = jnp.asarray(plan.depth_forward())
        self.inverse = jnp.asarray(plan.depth_inverse())
        slab, chan = lax.axis_index("slab"), lax.axis_index("chan")
        self.slab, self.chan = slab, chan
        turns = jnp.asarray(plan.turns())
        self.turn = lax.dynamic_index_in_dim(
            lax.dynamic_index_in_dim(turns, slab, 0, False), chan, 0, False
        )
        self.flag = (chan % 2).astype(jnp.int32).reshape(1)
        orders = jnp.asarray(plan.orders())
        upper = (chan >= plan.half).astype(jnp.int32)
        self.order = lax.dynamic_index_in_dim(orders, upper, 0, False)
        self.disorder = self.order.T
        chosen, back = plan.selections()
        self.chosen, self.back = jnp.asarray(chosen), jnp.asarray(back)
        self.matmul = 6 * plan.c * plan.rc * 2 * plan.lp * plan.nx * plan.ny
        self.field = plan.nx * plan.ny * plan.nz * plan.c * 4

    def half_shape(self):
        plan = self.plan
        return (plan.half, 2, plan.rt, plan.lp)

    def field_spec(self):
        plan = self.plan
        return leading((plan.xb, plan.c, plan.ny, plan.nz))

    def tables(self):
        plan = self.plan
        return [leading((plan.blk, 2 * plan.lp))] * 2

    def lines(self):
        plan = self.plan
        return pltpu.VMEM((plan.c, plan.rc, plan.blk), f32)

    def spectra(self):
        plan = self.plan
        rows = pltpu.VMEM((plan.c * plan.rc, 2 * plan.lp), bf16)
        return [pltpu.VMEM((plan.c, plan.rc, 2 * plan.lp), f32), rows, rows]

    def analyse(self, values):
        plan = self.plan
        half = self.half_shape()
        return call(
            partial(analyse_kernel, plan), "analyse", plan.nx // plan.xb,
            [scalar(), self.field_spec(), *self.tables(), whole(self.depth), whole(self.turn)],
            [whole_shape(half)] * 2, [shaped(*half)] * 2,
            [self.lines(), self.spectra()[0]], self.matmul, self.field,
        )(self.flag, values, *self.plane, self.depth, self.turn)

    def middle(self, own, other, linear, cotangent):
        plan = self.plan
        half = self.half_shape()
        field = shaped(plan.nx, plan.c, plan.ny, plan.nz)
        return call(
            partial(middle_kernel, plan), "middle", plan.nx // plan.xb,
            [scalar(), whole_shape(half), whole_shape(half), self.field_spec(), self.field_spec(), *self.tables(),
             whole(self.depth), whole(self.inverse), whole(self.turn)],
            [self.field_spec(), self.field_spec(), whole_shape(half), whole_shape(half)],
            [field, field, shaped(*half), shaped(*half)],
            [self.lines(), self.lines(), *self.spectra()], 2 * self.matmul, 4 * self.field,
        )(self.flag, own, other, linear, cotangent, *self.plane, self.depth, self.inverse, self.turn)

    def synthesise(self, own, other, linear):
        plan = self.plan
        half = self.half_shape()
        return call(
            partial(synthesise_kernel, plan), "synthesise", plan.nx // plan.xb,
            [scalar(), whole_shape(half), whole_shape(half), self.field_spec(), *self.tables(),
             whole(self.inverse), whole(self.turn)],
            self.field_spec(), shaped(plan.nx, plan.c, plan.ny, plan.nz),
            [self.lines(), *self.spectra()], self.matmul, 2 * self.field,
        )(self.flag, own, other, linear, *self.plane, self.inverse, self.turn)

    def linear(self, values, matrix, bias):
        plan = self.plan
        wide = jnp.kron(matrix, jnp.eye(8, dtype=f32))
        column = jnp.repeat(bias, 8)[:, None]
        spec = leading((1, plan.c, plan.ny, plan.nz))
        return call(
            partial(linear_kernel, plan), "linear", plan.nx,
            [spec, whole(wide), whole(column)],
            spec, shaped(plan.nx, plan.c, plan.ny, plan.nz), [],
            6 * (8 * plan.c) ** 2 * plan.nx * plan.ny // 8 * plan.nz, 2 * self.field,
        )(values, wide, column)

    def mix_specs(self):
        plan = self.plan
        modes = (plan.rt, plan.ll)
        ins = [
            whole_shape(modes), whole_shape(modes), whole(self.order), whole(self.disorder),
            leading((1,) + self.chosen.shape[1:]), leading((1,) + self.back.shape[1:]),
            leading((1, 2, plan.c, plan.wk, plan.c * plan.mx)),
        ]
        scratch = [
            pltpu.VMEM((plan.rows, 2 * plan.ll), f32),
            pltpu.VMEM((plan.rows, 256), f32),
            pltpu.VMEM((plan.rows, 2 * plan.ll), f32),
        ]
        return ins, [whole_shape(modes)] * 2, [shaped(*modes)] * 2, scratch

    def mix(self, own, mirror, weights):
        plan = self.plan
        ins, outs, shapes, scratch = self.mix_specs()
        kept = leading((1, plan.rows, 256))
        return call(
            partial(mix_kernel, plan), "mix", plan.wb, ins, [kept, *outs],
            [shaped(plan.wb, plan.rows, 256), *shapes], scratch, 10**9, 4 * weights.size,
        )(own, mirror, self.order, self.disorder, self.chosen, self.back, weights)

    def mix_back(self, own, mirror, weights, modes):
        plan = self.plan
        ins, outs, shapes, scratch = self.mix_specs()
        kept = leading((1, plan.rows, 256))
        return call(
            partial(mix_back_kernel, plan), "mix_back", plan.wb, ins + [kept], [ins[-1], *outs],
            [shaped(*weights.shape), *shapes], scratch, 10**9, 8 * weights.size,
        )(own, mirror, self.order, self.disorder, self.chosen, self.back, weights, modes)

    def across(self, value, axis, bit):
        size = lax.axis_size(axis)
        return lax.ppermute(value, axis, [(i, i ^ bit) for i in range(size)])

    def mirrored(self, value):
        total = self.plan.s * self.plan.ch
        return lax.ppermute(value, ("slab", "chan"), [(i, total - 1 - i) for i in range(total)])

    def gather_sums(self, keep, send):
        plan = self.plan
        total = keep + self.across(send, "chan", 1)
        bit = 2
        while bit < plan.ch:
            mine = (self.chan // bit) % 2
            pairs = total.reshape((total.shape[0] // 2, 2) + total.shape[1:])
            send = lax.dynamic_index_in_dim(pairs, 1 - mine, 1, False)
            total = lax.dynamic_index_in_dim(pairs, mine, 1, False) + self.across(send, "chan", bit)
            bit *= 2
        total = total[0]
        blank = jnp.zeros((plan.rt, plan.ll - 2 * plan.span), f32)
        pieces = []
        for g in range(plan.s):
            window = slice(g * plan.span, (g + 1) * plan.span)
            pieces.append(jnp.concatenate([total[0, :, window], total[1, :, window], blank], axis=1))
        pieces = jnp.stack(pieces)
        mine = lax.dynamic_index_in_dim(pieces, self.slab, 0, False)
        arrived = [
            self.across(lax.dynamic_index_in_dim(pieces, self.slab ^ j, 0, False), "slab", j)
            for j in range(1, plan.s)
        ]
        for piece in arrived:
            mine = mine + piece
        return mine, self.mirrored(mine)

    def spread_modes(self, own, mirror):
        plan = self.plan
        mine = own + self.mirrored(mirror)
        held = jnp.stack([mine] + [self.across(mine, "slab", j) for j in range(1, plan.s)])
        pieces = [lax.dynamic_index_in_dim(held, self.slab ^ g, 0, False) for g in range(plan.s)]
        blank = jnp.zeros((plan.rt, plan.lp - plan.lw), f32)
        total = jnp.stack([
            jnp.concatenate([p[:, r * plan.span : (r + 1) * plan.span] for p in pieces] + [blank], axis=1)
            for r in range(2)
        ])[None]
        bit = plan.ch // 2
        while bit > 1:
            other = self.across(total, "chan", bit)
            upper = (self.chan // bit) % 2 == 1
            total = jnp.stack([jnp.where(upper, other, total), jnp.where(upper, total, other)], axis=1)
            total = total.reshape((-1,) + total.shape[2:])
            bit //= 2
        return total, self.across(total, "chan", 1)


def local(inputs, cotangent, spectral, local_weight, bias_vector):
    nx, ny, channels, nz = inputs.shape
    wb, wk = spectral.shape[0], spectral.shape[1]
    plan = Plan(nx, ny, nz, channels, wb, wk, spectral.shape[4] // channels, lax.axis_size("slab"), lax.axis_size("chan"))
    program = Program(plan)
    values = jnp.transpose(inputs, (0, 2, 1, 3))
    weights = jnp.transpose(spectral, (0, 2, 3, 1, 4))
    own, mirror = program.gather_sums(*program.analyse(values))
    linear = program.linear(values, local_weight.T, bias_vector)
    modes, own, mirror = program.mix(own, mirror, weights)
    own, other = program.spread_modes(own, mirror)
    output, gradient, keep, send = program.middle(own, other, linear, jnp.transpose(cotangent, (0, 2, 1, 3)))
    own, mirror = program.gather_sums(keep, send)
    linear = program.linear(gradient, local_weight, jnp.zeros_like(bias_vector))
    grad_spectral, own, mirror = program.mix_back(own, mirror, weights, modes)
    own, other = program.spread_modes(own, mirror)
    grad_inputs = program.synthesise(own, other, linear)
    return (
        jnp.transpose(output, (0, 2, 1, 3)),
        jnp.transpose(grad_inputs, (0, 2, 1, 3)),
        jnp.transpose(grad_spectral, (0, 3, 1, 2, 4)),
    )


def solution(mesh):
    in_specs = (
        P(("groups", "slab"), "chan", None, None),
        P(("groups", "slab"), "chan", None, None),
        P("slab", "chan", None, None, None),
        P(),
        P(),
    )
    out_specs = (
        P(("groups", "slab"), "chan", None, None),
        P(("groups", "slab"), "chan", None, None),
        P(("groups", "slab"), "chan", None, None, None),
    )
    return jax.shard_map(local, mesh=mesh, in_specs=in_specs, out_specs=out_specs, check_vma=False)
```

time: 1230 us -> 522 us (0.42)
  matrix products: 340 us -> 0 us
  waiting for transfers between devices: 506 us -> 213 us
  Pallas kernels: 0 us -> 212 us
  local copies, waits for them, and re-layouts: 218 us -> 35.8 us
  blocking collectives: 82.4 us -> 0 us
  other arithmetic: 49.7 us -> 12.6 us
  starting transfers between devices: 10.3 us -> 45.1 us
  between operations: 14.6 us -> 0.86 us
    reduce_scatter x4 -> x0, waiting for transfers between devices: 468 us -> none  [the longest x2 307 us: forward_modes(): lax.psum_scatter(jnp.einsum('qpbn,knxpc->kbxqc', col_table, piece_rows, p...]
    dot_general x14 -> x0, matrix products: 340 us -> none  [the longest x2 112 us: forward_modes(): jnp.einsum('xycz,pkz->kyxpc', values, depth_table, precision=highest)]
    ppermute x0 -> x24, waiting for transfers between devices: none -> 213 us  [the longest x20 181 us: across(): return lax.ppermute(value, axis, [(i, i ^ bit) for i in range(size)])]
    pallas_call x0 -> x7, Pallas kernels: none -> 212 us  [the longest x1 67.4 us: middle(): call(partial(middle_kernel, plan), 'middle', plan.nx // plan.xb, [scalar(...]
    reshape x9 -> x0, local copies, waits for them, and re-layouts: 93.5 us -> none  [the longest x2 47.3 us: inverse_field(): planes = planes.reshape(MZ, rows_y, rows_x, 2, C)]
    all_to_all x2 -> x0, blocking collectives: 82.4 us -> none  [inverse_field(): lax.all_to_all(columns.reshape(second_local, NX, depth_local * 2 * C), 's...]
    all_to_all x4 -> x0, local copies, waits for them, and re-layouts: 46.4 us -> none  [the longest x2 35.1 us: inverse_field(): lax.all_to_all(planes.reshape(depth_local, NY, rows_x * 2 * C), 'chan', s...]
    ppermute x0 -> x24, starting transfers between devices: none -> 45.1 us  [the longest x20 41.9 us: across(): return lax.ppermute(value, axis, [(i, i ^ bit) for i in range(size)])]
  transfers between devices with their start and end apart: 6 -> 24, of which waited for: 5 -> 18; matrix products, arithmetic and copies ran while one was open for 11% -> 5% of each run, Pallas kernels for 0% -> 9%
where the time goes in v1:
time: 522 us; the launch traced here: 520 us
  waiting for transfers between devices  213 us (41%)
  Pallas kernels  212 us (41%)
  starting transfers between devices  45.1 us (9%)
  local copies, waits for them, and re-layouts  35.8 us (7%)
  other arithmetic  12.6 us (2%)
    ppermute x20, waiting for transfers between devices, across(): return lax.ppermute(value, axis, [(i, i ^ bit) for i in range(size)])  181 us
    pallas_call x1, Pallas kernels, middle(): call(partial(middle_kernel, plan), 'middle', plan.nx // plan.xb, [scalar(...  67.4 us
    pallas_call x2, Pallas kernels, linear(): call(partial(linear_kernel, plan), 'linear', plan.nx, [spec, whole(wide),...  48.2 us
    ppermute x20, starting transfers between devices, across(): return lax.ppermute(value, axis, [(i, i ^ bit) for i in range(size)])  41.9 us
    pallas_call x1, Pallas kernels, analyse(): call(partial(analyse_kernel, plan), 'analyse', plan.nx // plan.xb, [scala...  36.9 us
    ppermute x4, waiting for transfers between devices, mirrored(): lax.ppermute(value, ('slab', 'chan'), [(i, total - 1 - i) for i in range(...  32.6 us
    pallas_call x1, Pallas kernels, synthesise(): call(partial(synthesise_kernel, plan), 'synthesise', plan.nx // plan.xb,...  30.3 us
    unnamed x18, local copies, waits for them, and re-layouts  20.2 us
  transfers between devices with their start and end apart: 24, of which 18 were waited for; matrix products, arithmetic and copies ran while one was open for 5% of the time, Pallas kernels for 9%

profile of v1, /device:TPU:0, one launch (start us, length us, event | category | flops | bytes accessed | tf_op | source)
XLA Modules:
  0.0 519.5 jit_solution(13767939482764451032)
XLA Ops:
  1.9 36.9 %analyse.1 = (f32[2,2,184,640]{3,2,1,0:T(8,128)}, f32[2,2,184,640]{3,2,1,0:T(8,128)}) custom-call(s32[1]{0:T(128)} %bitcast.flag_ref, f32[32,20,32,128]{3,2,1,0:T(8,128)} %bitcast.148, bf16[1024,1280]{1,0:T(8,128)(2,1)} %constant.148.clone.high_ref, bf16[1024,1280]{1,0:T(8,128)(2,1)} %constant.149.clone.low_ref, bf16[80,256]{1,0:T(8,128)(2,1)} %constant.150.clone.depth_ref, ...), custom_call_target="tpu_custom_call" | custom-call | flops 6291456000 | bytes 10485760 | tf_op jit(solution)/shard_map/analyse/pallas_call | solution.py:488
  50.5 21.3 %collective-permute-done.1 = f32[1,2,184,640]{3,2,1,0:T(8,128)S(1)} collective-permute-done((f32[1,2,184,640]{3,2,1,0:T(8,128)}, f32[1,2,184,640]{3,2,1,0:T(8,128)S(1)}, u32[]{:S(2)}, u32[]{:S(2)}) %collective-permute-start.1) | collective-permute-done | bytes 942112 | tf_op jit(solution)/shard_map/ppermute | solution.py:566
  81.8 9.1 %collective-permute-done.4 = f32[184,384]{1,0:T(8,128)S(1)} collective-permute-done((f32[184,384]{1,0:T(8,128)S(1)}, f32[184,384]{1,0:T(8,128)S(1)}, u32[]{:S(2)}, u32[]{:S(2)}) %collective-permute-start.4) | collective-permute-done | bytes 282656 | tf_op jit(solution)/shard_map/ppermute | solution.py:566
  90.9 10.4 %collective-permute-done.3 = f32[184,384]{1,0:T(8,128)S(1)} collective-permute-done((f32[184,384]{1,0:T(8,128)S(1)}, f32[184,384]{1,0:T(8,128)S(1)}, u32[]{:S(2)}, u32[]{:S(2)}) %collective-permute-start.3) | collective-permute-done | bytes 282656 | tf_op jit(solution)/shard_map/ppermute | solution.py:566
  104.1 6.8 %copy.28 = f32[8,8,2,20,640]{4,1,3,2,0:T(8,128)} copy(f32[8,8,2,20,640]{4,2,3,1,0:T(2,128)} %param.15) | data formatting | bytes 13107200 | tf_op args[2]
  113.4 13.7 %mix.1 = (f32[8,160,256]{2,1,0:T(8,128)}, f32[184,384]{1,0:T(8,128)}, f32[184,384]{1,0:T(8,128)}) custom-call(f32[184,384]{1,0:T(8,128)} %copy-done.1, f32[184,384]{1,0:T(8,128)} %copy-done.3, bf16[160,184]{1,0:T(8,128)(2,1)} %copy.22.order_ref, bf16[184,160]{1,0:T(8,128)(2,1)} %get-tuple-element.83.disorder_ref, ...), custom_call_target="tpu_custom_call" | custom-call | flops 1000000000 | bytes 6553600 | tf_op jit(solution)/shard_map/mix/pallas_call | solution.py:550
  128.5 9.9 %collective-permute-done.6 = f32[184,384]{1,0:T(8,128)S(1)} collective-permute-done((f32[184,384]{1,0:T(8,128)}, f32[184,384]{1,0:T(8,128)S(1)}, u32[]{:S(2)}, u32[]{:S(2)}) %collective-permute-start.6) | collective-permute-done | bytes 282656 | tf_op jit(solution)/shard_map/ppermute | solution.py:570
  141.3 13.0 %collective-permute-start.8 = (f32[184,384]{1,0:T(8,128)S(1)}, f32[184,384]{1,0:T(8,128)S(1)}, u32[]{:S(2)}, u32[]{:S(2)}) collective-permute-start(f32[184,384]{1,0:T(8,128)S(1)} %add.111), channel_id=1, source_target_pairs={{0,8},{4,12},{8,0},{12,4},{1,9},{5,13},{9,1},{13,5},{2,10},{6,14},... | collective-permute-start | bytes 847880 | tf_op jit(solution)/shard_map/ppermute | solution.py:566
  154.3 18.8 %collective-permute-done.8 = f32[184,384]{1,0:T(8,128)S(1)} collective-permute-done((f32[184,384]{1,0:T(8,128)S(1)}, f32[184,384]{1,0:T(8,128)S(1)}, u32[]{:S(2)}, u32[]{:S(2)}) %collective-permute-start.8) | collective-permute-done | bytes 282656 | tf_op jit(solution)/shard_map/ppermute | solution.py:566
  174.4 22.0 %collective-permute-done.10 = f32[1,2,184,640]{3,2,1,0:T(8,128)S(1)} collective-permute-done((f32[1,2,184,640]{3,2,1,0:T(8,128)S(1)}, f32[1,2,184,640]{3,2,1,0:T(8,128)S(1)}, u32[]{:S(2)}, u32[]{:S(2)}) %collective-permute-start.10) | collective-permute-done | bytes 942112 | tf_op jit(solution)/shard_map/ppermute | solution.py:566
  203.2 24.1 %linear.2.linear_ref = f32[32,20,32,128]{3,2,1,0:T(8,128)} custom-call(f32[32,20,32,128]{3,2,1,0:T(8,128)} %bitcast.149, f32[160,160]{1,0:T(8,128)} %mul.44.matrix_ref, f32[160,1]{1,0:T(8,128)} %broadcast_in_dim_reshape.8.bias_ref), custom_call_target="tpu_custom_call" | custom-call | flops 2516582400 | bytes 20971520 | tf_op jit(solution)/shard_map/linear/pallas_call | solution.py:524
  227.4 67.4 %middle.1 = (f32[32,20,32,128]{3,2,1,0:T(8,128)}, f32[32,20,32,128]{3,2,1,0:T(8,128)}, f32[2,2,184,640]{3,2,1,0:T(8,128)}, f32[2,2,184,640]{3,2,1,0:T(8,128)}) custom-call(s32[1]{0:T(128)} %bitcast.flag_ref, f32[2,2,184,640]{3,2,1,0:T(8,128)} %maximum_bitcast_fusion.own_ref, f32[2,2,184,640]{3,2,1,0:T(8,128)} %collective-permute-done.11.other_ref, ...), custom_call_target="tpu_custom_call" | custom-call | flops 12582912000 | bytes 41943040 | tf_op jit(solution)/shard_map/middle/pallas_call | solution.py:499
  301.3 22.9 %collective-permute-done.13 = f32[1,2,184,640]{3,2,1,0:T(8,128)S(1)} collective-permute-done((f32[1,2,184,640]{3,2,1,0:T(8,128)S(1)}, f32[1,2,184,640]{3,2,1,0:T(8,128)S(1)}, u32[]{:S(2)}, u32[]{:S(2)}) %collective-permute-start.13) | collective-permute-done | bytes 942112 | tf_op jit(solution)/shard_map/ppermute | solution.py:566
  328.7 10.2 %collective-permute-done.14 = f32[184,384]{1,0:T(8,128)S(1)} collective-permute-done((f32[184,384]{1,0:T(8,128)S(1)}, f32[184,384]{1,0:T(8,128)S(1)}, u32[]{:S(2)}, u32[]{:S(2)}) %collective-permute-start.14) | collective-permute-done | bytes 282656 | tf_op jit(solution)/shard_map/ppermute | solution.py:566
  340.5 12.2 %collective-permute-done.15 = f32[184,384]{1,0:T(8,128)S(1)} collective-permute-done((f32[184,384]{1,0:T(8,128)S(1)}, f32[184,384]{1,0:T(8,128)S(1)}, u32[]{:S(2)}, u32[]{:S(2)}) %collective-permute-start.15) | collective-permute-done | bytes 282656 | tf_op jit(solution)/shard_map/ppermute | solution.py:566
  352.9 10.4 %collective-permute-done.17.mirror_ref = f32[184,384]{1,0:T(8,128)S(1)} collective-permute-done((f32[184,384]{1,0:T(8,128)S(1)}, f32[184,384]{1,0:T(8,128)S(1)}, u32[]{:S(2)}, u32[]{:S(2)}) %collective-permute-start.17) | collective-permute-done | bytes 282656 | tf_op jit(solution)/shard_map/ppermute | solution.py:570
  364.0 15.4 %mix_back.1 = (f32[8,2,20,8,640]{4,3,2,1,0:T(8,128)}, f32[184,384]{1,0:T(8,128)}, f32[184,384]{1,0:T(8,128)}) custom-call(f32[184,384]{1,0:T(8,128)} %copy-done.2, f32[184,384]{1,0:T(8,128)} %copy-done.4, bf16[160,184]{1,0:T(8,128)(2,1)} %copy.22.order_ref, bf16[184,160]{1,0:T(8,128)(2,1)} %get-tuple-element.83.disorder_ref, ...), custom_call_target="tpu_custom_call" | custom-call | flops 1000000000 | bytes 13107200 | tf_op jit(solution)/shard_map/mix_back/pallas_call | solution.py:559
  379.7 10.5 %collective-permute-done.18 = f32[184,384]{1,0:T(8,128)S(1)} collective-permute-done((f32[184,384]{1,0:T(8,128)}, f32[184,384]{1,0:T(8,128)S(1)}, u32[]{:S(2)}, u32[]{:S(2)}) %collective-permute-start.18) | collective-permute-done | bytes 282656 | tf_op jit(solution)/shard_map/ppermute | solution.py:570
  392.9 12.4 %collective-permute-start.20 = (f32[184,384]{1,0:T(8,128)S(1)}, f32[184,384]{1,0:T(8,128)S(1)}, u32[]{:S(2)}, u32[]{:S(2)}) collective-permute-start(f32[184,384]{1,0:T(8,128)S(1)} %add.117), channel_id=1, source_target_pairs={{0,8},{4,12},{8,0},{12,4},{1,9},{5,13},{9,1},{13,5},{2,10},{6,14},... | collective-permute-start | bytes 847880 | tf_op jit(solution)/shard_map/ppermute | solution.py:566
  405.3 18.8 %collective-permute-done.20 = f32[184,384]{1,0:T(8,128)S(1)} collective-permute-done((f32[184,384]{1,0:T(8,128)S(1)}, f32[184,384]{1,0:T(8,128)S(1)}, u32[]{:S(2)}, u32[]{:S(2)}) %collective-permute-start.20) | collective-permute-done | bytes 282656 | tf_op jit(solution)/shard_map/ppermute | solution.py:566
  429.5 21.5 %collective-permute-done.22 = f32[1,2,184,640]{3,2,1,0:T(8,128)S(1)} collective-permute-done((f32[1,2,184,640]{3,2,1,0:T(8,128)S(1)}, f32[1,2,184,640]{3,2,1,0:T(8,128)S(1)}, u32[]{:S(2)}, u32[]{:S(2)}) %collective-permute-start.22) | collective-permute-done | bytes 942112 | tf_op jit(solution)/shard_map/ppermute | solution.py:566
  454.5 24.1 %linear.3.linear_ref = f32[32,20,32,128]{3,2,1,0:T(8,128)} custom-call(f32[32,20,32,128]{3,2,1,0:T(8,128)} %get-tuple-element.25.values_ref, f32[160,160]{1,0:T(8,128)} %mul.47.matrix_ref, f32[160,1]{1,0:T(8,128)} %broadcast_in_dim_reshape.7.bias_ref), custom_call_target="tpu_custom_call" | custom-call | flops 2516582400 | bytes 20971520 | tf_op jit(solution)/shard_map/linear/pallas_call | solution.py:524
  478.6 10.7 %copy.26 = f32[8,8,2,20,640]{4,2,3,1,0:T(2,128)} copy(f32[8,8,2,20,640]{4,1,3,2,0:T(8,128)} %bitcast.150) | data formatting | bytes 13107200
  489.3 30.3 %synthesise.1 = f32[32,20,32,128]{3,2,1,0:T(8,128)} custom-call(s32[1]{0:T(128)} %bitcast.flag_ref, f32[2,2,184,640]{3,2,1,0:T(8,128)} %maximum_bitcast_fusion.1.own_ref, f32[2,2,184,640]{3,2,1,0:T(8,128)} %collective-permute-done.23.other_ref, f32[32,20,32,128]{3,2,1,0:T(8,128)} %linear.3.linear_ref, bf16[1024,1280]{1,0:T(8,128)(2,1)} %constant.148.clone.high_ref, ...), custom_call_target="tpu_custom_call" | custom-call | flops 6291456000 | bytes 20971520 | tf_op jit(solution)/shard_map/synthesise/pallas_call | solution.py:511
  (101 shorter events, 65.9 us)
Async XLA Ops:
  38.9 4.1 collective-permute-start
  47.5 24.2 %collective-permute-start.1 = (f32[1,2,184,640]{3,2,1,0:T(8,128)}, f32[1,2,184,640]{3,2,1,0:T(8,128)S(1)}, u32[]{:S(2)}, u32[]{:S(2)}) collective-permute-start(f32[1,2,184,640]{3,2,1,0:T(8,128)} %constant_dynamic-slice_fusion.1), channel_id=1, source_target_pairs={{0,2},{1,3},{2,0},{3,1},{4,6},{5,7},{6,4},{7,5},{8,10},{9,11},{10,... | collective-permute-start | bytes 2826248 | tf_op jit(solution)/shard_map/ppermute | solution.py:566
  72.7 9.1 %collective-permute-start.2 = (f32[184,384]{1,0:T(8,128)S(1)}, f32[184,384]{1,0:T(8,128)S(1)}, u32[]{:S(2)}, u32[]{:S(2)}) collective-permute-start(f32[184,384]{1,0:T(8,128)S(1)} %get-tuple-element.48), channel_id=1, source_target_pairs={{0,4},{4,0},{8,12},{12,8},{1,5},{5,1},{9,13},{13,9},{2,6},{6,2},{1... | collective-permute-start | bytes 847880 | tf_op jit(solution)/shard_map/ppermute | solution.py:566
  74.6 16.3 %collective-permute-start.4 = (f32[184,384]{1,0:T(8,128)S(1)}, f32[184,384]{1,0:T(8,128)S(1)}, u32[]{:S(2)}, u32[]{:S(2)}) collective-permute-start(f32[184,384]{1,0:T(8,128)S(1)} %get-tuple-element.49), channel_id=1, source_target_pairs={{0,12},{4,8},{8,4},{12,0},{1,13},{5,9},{9,5},{13,1},{2,14},{6,10},... | collective-permute-start | bytes 847880 | tf_op jit(solution)/shard_map/ppermute | solution.py:566
  77.1 24.2 %collective-permute-start.3 = (f32[184,384]{1,0:T(8,128)S(1)}, f32[184,384]{1,0:T(8,128)S(1)}, u32[]{:S(2)}, u32[]{:S(2)}) collective-permute-start(f32[184,384]{1,0:T(8,128)S(1)} %get-tuple-element.50), channel_id=1, source_target_pairs={{0,8},{4,12},{8,0},{12,4},{1,9},{5,13},{9,1},{13,5},{2,10},{6,14},... | collective-permute-start | bytes 847880 | tf_op jit(solution)/shard_map/ppermute | solution.py:566
  101.4 11.3 %collective-permute-start.5 = (f32[184,384]{1,0:T(8,128)S(1)}, f32[184,384]{1,0:T(8,128)S(1)}, u32[]{:S(2)}, u32[]{:S(2)}) collective-permute-start(f32[184,384]{1,0:T(8,128)S(1)} %fusion.3.own_ref), channel_id=1, source_target_pairs={{0,15},{1,14},{2,13},{3,12},{4,11},{5,10},{6,9},{7,8},{8,7},{9,6},... | collective-permute-start | bytes 847880 | tf_op jit(solution)/shard_map/ppermute | solution.py:570
  127.1 11.3 %collective-permute-start.6 = (f32[184,384]{1,0:T(8,128)}, f32[184,384]{1,0:T(8,128)S(1)}, u32[]{:S(2)}, u32[]{:S(2)}) collective-permute-start(f32[184,384]{1,0:T(8,128)} %get-tuple-element.18), channel_id=1, source_target_pairs={{0,15},{1,14},{2,13},{3,12},{4,11},{5,10},{6,9},{7,8},{8,7},{9,6},... | collective-permute-start | bytes 847880 | tf_op jit(solution)/shard_map/ppermute | solution.py:570
  139.4 14.9 %collective-permute-start.9 = (f32[184,384]{1,0:T(8,128)S(1)}, f32[184,384]{1,0:T(8,128)S(1)}, u32[]{:S(2)}, u32[]{:S(2)}) collective-permute-start(f32[184,384]{1,0:T(8,128)S(1)} %add.111), channel_id=1, source_target_pairs={{0,12},{4,8},{8,4},{12,0},{1,13},{5,9},{9,5},{13,1},{2,14},{6,10},... | collective-permute-start | bytes 847880 | tf_op jit(solution)/shard_map/ppermute | solution.py:566
  141.3 31.8 %collective-permute-start.8 = (f32[184,384]{1,0:T(8,128)S(1)}, f32[184,384]{1,0:T(8,128)S(1)}, u32[]{:S(2)}, u32[]{:S(2)}) collective-permute-start(f32[184,384]{1,0:T(8,128)S(1)} %add.111), channel_id=1, source_target_pairs={{0,8},{4,12},{8,0},{12,4},{1,9},{5,13},{9,1},{13,5},{2,10},{6,14},... | collective-permute-start | bytes 847880 | tf_op jit(solution)/shard_map/ppermute | solution.py:566
  154.3 18.8 %collective-permute-start.7 = (f32[184,384]{1,0:T(8,128)S(1)}, f32[184,384]{1,0:T(8,128)S(1)}, u32[]{:S(2)}, u32[]{:S(2)}) collective-permute-start(f32[184,384]{1,0:T(8,128)S(1)} %add.111), channel_id=1, source_target_pairs={{0,4},{4,0},{8,12},{12,8},{1,5},{5,1},{9,13},{13,9},{2,6},{6,2},{1... | collective-permute-start | bytes 847880 | tf_op jit(solution)/shard_map/ppermute | solution.py:566
  174.3 22.1 %collective-permute-start.10 = (f32[1,2,184,640]{3,2,1,0:T(8,128)S(1)}, f32[1,2,184,640]{3,2,1,0:T(8,128)S(1)}, u32[]{:S(2)}, u32[]{:S(2)}) collective-permute-start(f32[1,2,184,640]{3,2,1,0:T(8,128)S(1)} %maximum_bitcast_fusion.2), channel_id=1, source_target_pairs={{0,2},{1,3},{2,0},{3,1},{4,6},{5,7},{6,4},{7,5},{8,10},{9,11},{10,... | collective-permute-start | bytes 2826248 | tf_op jit(solution)/shard_map/ppermute | solution.py:566
  198.1 29.3 %collective-permute-start.11 = (f32[2,2,184,640]{3,2,1,0:T(8,128)}, f32[2,2,184,640]{3,2,1,0:T(8,128)}, u32[]{:S(2)}, u32[]{:S(2)}) collective-permute-start(f32[2,2,184,640]{3,2,1,0:T(8,128)} %maximum_bitcast_fusion.own_ref), channel_id=1, source_target_pairs={{0,1},{1,0},{2,3},{3,2},{4,5},{5,4},{6,7},{7,6},{8,9},{9,8},{10,11... | collective-permute-start | bytes 5652488 | tf_op jit(solution)/shard_map/ppermute | solution.py:566
  294.8 4.3 collective-permute-start.12
  301.0 23.2 %collective-permute-start.13 = (f32[1,2,184,640]{3,2,1,0:T(8,128)S(1)}, f32[1,2,184,640]{3,2,1,0:T(8,128)S(1)}, u32[]{:S(2)}, u32[]{:S(2)}) collective-permute-start(f32[1,2,184,640]{3,2,1,0:T(8,128)S(1)} %constant_dynamic-slice_fusion), channel_id=1, source_target_pairs={{0,2},{1,3},{2,0},{3,1},{4,6},{5,7},{6,4},{7,5},{8,10},{9,11},{10,... | collective-permute-start | bytes 2826248 | tf_op jit(solution)/shard_map/ppermute | solution.py:566
  325.1 13.8 %collective-permute-start.14 = (f32[184,384]{1,0:T(8,128)S(1)}, f32[184,384]{1,0:T(8,128)S(1)}, u32[]{:S(2)}, u32[]{:S(2)}) collective-permute-start(f32[184,384]{1,0:T(8,128)S(1)} %get-tuple-element.41), channel_id=1, source_target_pairs={{0,4},{4,0},{8,12},{12,8},{1,5},{5,1},{9,13},{13,9},{2,6},{6,2},{1... | collective-permute-start | bytes 847880 | tf_op jit(solution)/shard_map/ppermute | solution.py:566
  325.2 15.3 %collective-permute-start.16 = (f32[184,384]{1,0:T(8,128)S(1)}, f32[184,384]{1,0:T(8,128)S(1)}, u32[]{:S(2)}, u32[]{:S(2)}) collective-permute-start(f32[184,384]{1,0:T(8,128)S(1)} %get-tuple-element.42), channel_id=1, source_target_pairs={{0,12},{4,8},{8,4},{12,0},{1,13},{5,9},{9,5},{13,1},{2,14},{6,10},... | collective-permute-start | bytes 847880 | tf_op jit(solution)/shard_map/ppermute | solution.py:566
  326.9 25.9 %collective-permute-start.15 = (f32[184,384]{1,0:T(8,128)S(1)}, f32[184,384]{1,0:T(8,128)S(1)}, u32[]{:S(2)}, u32[]{:S(2)}) collective-permute-start(f32[184,384]{1,0:T(8,128)S(1)} %get-tuple-element.43), channel_id=1, source_target_pairs={{0,8},{4,12},{8,0},{12,4},{1,9},{5,13},{9,1},{13,5},{2,10},{6,14},... | collective-permute-start | bytes 847880 | tf_op jit(solution)/shard_map/ppermute | solution.py:566
  352.8 10.4 %collective-permute-start.17 = (f32[184,384]{1,0:T(8,128)S(1)}, f32[184,384]{1,0:T(8,128)S(1)}, u32[]{:S(2)}, u32[]{:S(2)}) collective-permute-start(f32[184,384]{1,0:T(8,128)S(1)} %fusion.1.own_ref), channel_id=1, source_target_pairs={{0,15},{1,14},{2,13},{3,12},{4,11},{5,10},{6,9},{7,8},{8,7},{9,6},... | collective-permute-start | bytes 847880 | tf_op jit(solution)/shard_map/ppermute | solution.py:570
  379.4 10.9 %collective-permute-start.18 = (f32[184,384]{1,0:T(8,128)}, f32[184,384]{1,0:T(8,128)S(1)}, u32[]{:S(2)}, u32[]{:S(2)}) collective-permute-start(f32[184,384]{1,0:T(8,128)} %get-tuple-element.24), channel_id=1, source_target_pairs={{0,15},{1,14},{2,13},{3,12},{4,11},{5,10},{6,9},{7,8},{8,7},{9,6},... | collective-permute-start | bytes 847880 | tf_op jit(solution)/shard_map/ppermute | solution.py:570
  391.2 14.1 %collective-permute-start.21 = (f32[184,384]{1,0:T(8,128)S(1)}, f32[184,384]{1,0:T(8,128)S(1)}, u32[]{:S(2)}, u32[]{:S(2)}) collective-permute-start(f32[184,384]{1,0:T(8,128)S(1)} %add.117), channel_id=1, source_target_pairs={{0,12},{4,8},{8,4},{12,0},{1,13},{5,9},{9,5},{13,1},{2,14},{6,10},... | collective-permute-start | bytes 847880 | tf_op jit(solution)/shard_map/ppermute | solution.py:566
  392.9 31.3 %collective-permute-start.20 = (f32[184,384]{1,0:T(8,128)S(1)}, f32[184,384]{1,0:T(8,128)S(1)}, u32[]{:S(2)}, u32[]{:S(2)}) collective-permute-start(f32[184,384]{1,0:T(8,128)S(1)} %add.117), channel_id=1, source_target_pairs={{0,8},{4,12},{8,0},{12,4},{1,9},{5,13},{9,1},{13,5},{2,10},{6,14},... | collective-permute-start | bytes 847880 | tf_op jit(solution)/shard_map/ppermute | solution.py:566
  405.3 18.8 %collective-permute-start.19 = (f32[184,384]{1,0:T(8,128)S(1)}, f32[184,384]{1,0:T(8,128)S(1)}, u32[]{:S(2)}, u32[]{:S(2)}) collective-permute-start(f32[184,384]{1,0:T(8,128)S(1)} %add.117), channel_id=1, source_target_pairs={{0,4},{4,0},{8,12},{12,8},{1,5},{5,1},{9,13},{13,9},{2,6},{6,2},{1... | collective-permute-start | bytes 847880 | tf_op jit(solution)/shard_map/ppermute | solution.py:566
  428.9 22.1 %collective-permute-start.22 = (f32[1,2,184,640]{3,2,1,0:T(8,128)S(1)}, f32[1,2,184,640]{3,2,1,0:T(8,128)S(1)}, u32[]{:S(2)}, u32[]{:S(2)}) collective-permute-start(f32[1,2,184,640]{3,2,1,0:T(8,128)S(1)} %maximum_bitcast_fusion.3), channel_id=1, source_target_pairs={{0,2},{1,3},{2,0},{3,1},{4,6},{5,7},{6,4},{7,5},{8,10},{9,11},{10,... | collective-permute-start | bytes 2826248 | tf_op jit(solution)/shard_map/ppermute | solution.py:566
  452.6 36.6 %collective-permute-start.23 = (f32[2,2,184,640]{3,2,1,0:T(8,128)}, f32[2,2,184,640]{3,2,1,0:T(8,128)}, u32[]{:S(2)}, u32[]{:S(2)}) collective-permute-start(f32[2,2,184,640]{3,2,1,0:T(8,128)} %maximum_bitcast_fusion.1.own_ref), channel_id=1, source_target_pairs={{0,1},{1,0},{2,3},{3,2},{4,5},{5,4},{6,7},{7,6},{8,9},{9,8},{10,11... | collective-permute-start | bytes 5652488 | tf_op jit(solution)/shard_map/ppermute | solution.py:566
  (8 other events, 55.9 us)

commit v2 on v1

--- a/solution.py
+++ b/solution.py
@@ -40,6 +40,8 @@
         self.xb = math.gcd(8, nx)
         self.blk = self.xb * ny
         self.rows = channels * wk
+        self.lb = math.gcd(4, nx)
+        self.batch = max(d for d in range(1, 5) if channels % d == 0)
         self.full_x, self.full_y = nx * slab_count, ny * chan_count
 
     def starts(self):
@@ -61,7 +63,8 @@
         scale = 1.0 / math.sqrt(total)
         table[:, : self.lw] = np.cos(phase) * scale
         table[:, self.lp : self.lp + self.lw] = -np.sin(phase) * scale
-        return halves(table)
+        high, low = (t.reshape(self.nx // self.xb, 1, self.blk, 2 * self.lp) for t in halves(table))
+        return np.concatenate([high, high, low], 1).reshape(-1, 3 * self.blk, 2 * self.lp)
 
     def turns(self):
         a, b = self.columns()
@@ -139,19 +142,24 @@
 
 
 def moved(value, chosen, left=False):
-    first = value.astype(bf16)
-    rest = value - first.astype(f32)
-    second = rest.astype(bf16)
-    third = (rest - second.astype(f32)).astype(bf16)
+    first, second = split(value)
     if left:
-        return dot(chosen, first) + dot(chosen, second) + dot(chosen, third)
-    return dot(first, chosen) + dot(second, chosen) + dot(third, chosen)
+        return dot(chosen, first) + dot(chosen, second)
+    rows = value.shape[0]
+    if rows % 16:
+        return dot(first, chosen) + dot(second, chosen)
+    both = dot(jnp.concatenate([first, second], axis=0), chosen)
+    return both[:rows] + both[rows:]
 
 
 def depth_analysis(plan, table_ref, values):
-    high, low = split(values)
-    both = dot(table_ref[...], jnp.concatenate([high, low], axis=1), NT)
-    return both[: plan.rc] + both[plan.rc :]
+    rows = []
+    for value in values:
+        high, low = split(value)
+        rows.append(jnp.concatenate([high, low], axis=1))
+    both = dot(table_ref[...], jnp.concatenate(rows, axis=0), NT)
+    lines = both[: plan.rc] + both[plan.rc :]
+    return [lines[:, j * plan.blk : (j + 1) * plan.blk] for j in range(len(values))]
 
 
 def depth_synthesis(plan, table_ref, rows):
@@ -163,13 +171,13 @@
     return dot(jnp.concatenate(parts, axis=0).astype(bf16), table_ref[...], TN)
 
 
-def plane_analysis(plan, step, lines_ref, high_ref, low_ref, total_ref):
+def plane_analysis(plan, step, lines_ref, plane_ref, total_ref):
     high, low = split(lines_ref[...].reshape(plan.c * plan.rc, plan.blk))
+    rows = jnp.concatenate([high, low, high], axis=1)
     for start in range(0, 2 * plan.lp, 256):
         size = min(256, 2 * plan.lp - start)
         columns = pl.ds(start, size)
-        part = dot(high, high_ref[:, columns]) + dot(low, high_ref[:, columns]) + dot(high, low_ref[:, columns])
-        part = part.reshape(plan.c, plan.rc, size)
+        part = dot(rows, plane_ref[0, :, columns]).reshape(plan.c, plan.rc, size)
 
         @pl.when(step == 0)
         def _():
@@ -180,8 +188,8 @@
             total_ref[:, :, columns] += part
 
 
-def plane_synthesis(plan, high_rows, low_rows, high_ref, low_ref, lines_ref):
-    high_table, low_table = high_ref[...], low_ref[...]
+def plane_synthesis(plan, high_rows, low_rows, plane_ref, lines_ref):
+    high_table, low_table = plane_ref[0, : plan.blk], plane_ref[0, 2 * plan.blk :]
     lines = (
         dot(high_rows[...], high_table, NT)
         + dot(low_rows[...], high_table, NT)
@@ -250,22 +258,30 @@
     low_rows[...] = low
 
 
-def analyse_kernel(plan, flag_ref, values_ref, high_ref, low_ref, depth_ref, turn_ref, keep_ref, send_ref, lines_ref, total_ref):
+def analyse_kernel(plan, flag_ref, values_ref, plane_ref, depth_ref, turn_ref, keep_ref, send_ref, lines_ref, total_ref):
     step = pl.program_id(0)
 
-    @pl.loop(0, plan.c)
+    @pl.loop(0, plan.c, step=plan.batch)
     def _(c):
-        lines_ref[c] = depth_analysis(plan, depth_ref, values_ref[:, c].reshape(plan.blk, plan.nz))
-
-    plane_analysis(plan, step, lines_ref, high_ref, low_ref, total_ref)
+        values = [values_ref[:, c + j].reshape(plan.blk, plan.nz) for j in range(plan.batch)]
+        for j, lines in enumerate(depth_analysis(plan, depth_ref, values)):
+            lines_ref[c + j] = lines
+
+    plane_analysis(plan, step, lines_ref, plane_ref, total_ref)
 
     @pl.when(step == pl.num_programs(0) - 1)
     def _():
         emit_modes(plan, flag_ref, turn_ref, total_ref, keep_ref, send_ref)
 
 
+def fields(plan, inverse_ref, lines_ref, first):
+    lines = jnp.concatenate([lines_ref[first + j] for j in range(plan.batch)], axis=1)
+    values = depth_synthesis(plan, inverse_ref, lines)
+    return [values[j * plan.blk : (j + 1) * plan.blk] for j in range(plan.batch)]
+
+
 def middle_kernel(
-    plan, flag_ref, own_ref, other_ref, linear_ref, cotangent_ref, high_ref, low_ref, depth_ref, inverse_ref, turn_ref,
+    plan, flag_ref, own_ref, other_ref, linear_ref, cotangent_ref, plane_ref, depth_ref, inverse_ref, turn_ref,
     output_ref, gradient_ref, keep_ref, send_ref, lines_ref, back_ref, total_ref, high_rows, low_rows,
 ):
     step = pl.program_id(0)
@@ -274,21 +290,23 @@
     def _():
         take_modes(plan, flag_ref, turn_ref, own_ref, other_ref, total_ref, high_rows, low_rows)
 
-    plane_synthesis(plan, high_rows, low_rows, high_ref, low_ref, lines_ref)
+    plane_synthesis(plan, high_rows, low_rows, plane_ref, lines_ref)
     shape = (plan.xb, plan.ny, plan.nz)
 
-    @pl.loop(0, plan.c)
-    def _(o):
-        field = depth_synthesis(plan, inverse_ref, lines_ref[o])
-        value = field + linear_ref[:, o].reshape(plan.blk, plan.nz)
-        gate = 0.5 * (1.0 + lax.erf(value * root_half))
-        slope = gate + value * jnp.exp(-0.5 * value * value) * inv_root_two_pi
-        output_ref[:, o] = (value * gate).reshape(shape)
-        gradient = cotangent_ref[:, o].reshape(plan.blk, plan.nz) * slope
-        gradient_ref[:, o] = gradient.reshape(shape)
-        back_ref[o] = depth_analysis(plan, depth_ref, gradient)
-
-    plane_analysis(plan, step, back_ref, high_ref, low_ref, total_ref)
+    @pl.loop(0, plan.c, step=plan.batch)
+    def _(first):
+        gradients = []
+        for j, field in enumerate(fields(plan, inverse_ref, lines_ref, first)):
+            value = field + linear_ref[:, first + j].reshape(plan.blk, plan.nz)
+            gate = 0.5 * (1.0 + lax.erf(value * root_half))
+            slope = gate + value * jnp.exp(-0.5 * value * value) * inv_root_two_pi
+            output_ref[:, first + j] = (value * gate).reshape(shape)
+            gradients.append(cotangent_ref[:, first + j].reshape(plan.blk, plan.nz) * slope)
+            gradient_ref[:, first + j] = gradients[-1].reshape(shape)
+        for j, lines in enumerate(depth_analysis(plan, depth_ref, gradients)):
+            back_ref[first + j] = lines
+
+    plane_analysis(plan, step, back_ref, plane_ref, total_ref)
 
     @pl.when(step == pl.num_programs(0) - 1)
     def _():
@@ -296,29 +314,31 @@
 
 
 def synthesise_kernel(
-    plan, flag_ref, own_ref, other_ref, linear_ref, high_ref, low_ref, inverse_ref, turn_ref,
+    plan, flag_ref, own_ref, other_ref, linear_ref, plane_ref, inverse_ref, turn_ref,
     output_ref, lines_ref, total_ref, high_rows, low_rows,
 ):
     @pl.when(pl.program_id(0) == 0)
     def _():
         take_modes(plan, flag_ref, turn_ref, own_ref, other_ref, total_ref, high_rows, low_rows)
 
-    plane_synthesis(plan, high_rows, low_rows, high_ref, low_ref, lines_ref)
-
-    @pl.loop(0, plan.c)
-    def _(o):
-        value = depth_synthesis(plan, inverse_ref, lines_ref[o]) + linear_ref[:, o].reshape(plan.blk, plan.nz)
-        output_ref[:, o] = value.reshape(plan.xb, plan.ny, plan.nz)
-
-
-def linear_kernel(plan, values_ref, matrix_ref, bias_ref, output_ref):
-    tiles = plan.ny // 8
-    values = [values_ref[0, :, t * 8 : (t + 1) * 8, :].reshape(plan.c * 8, plan.nz) for t in range(tiles)]
+    plane_synthesis(plan, high_rows, low_rows, plane_ref, lines_ref)
+
+    @pl.loop(0, plan.c, step=plan.batch)
+    def _(first):
+        for j, field in enumerate(fields(plan, inverse_ref, lines_ref, first)):
+            value = field + linear_ref[:, first + j].reshape(plan.blk, plan.nz)
+            output_ref[:, first + j] = value.reshape(plan.xb, plan.ny, plan.nz)
+
+
+def linear_kernel(plan, after_ref, values_ref, matrix_ref, bias_ref, output_ref):
+    tiles = [(x, slice(t * 8, (t + 1) * 8)) for x in range(plan.lb) for t in range(plan.ny // 8)]
+    values = [values_ref[x, :, t, :].reshape(plan.c * 8, plan.nz) for x, t in tiles]
     high, low = split(jnp.concatenate(values, axis=1))
     high_matrix, low_matrix = split(matrix_ref[...])
-    mixed = dot(high_matrix, high) + dot(high_matrix, low) + dot(low_matrix, high) + bias_ref[...]
-    for t in range(tiles):
-        output_ref[0, :, t * 8 : (t + 1) * 8, :] = mixed[:, t * plan.nz : (t + 1) * plan.nz].reshape(plan.c, 8, plan.nz)
+    matrix = jnp.concatenate([high_matrix, high_matrix, low_matrix], axis=1)
+    mixed = dot(matrix, jnp.concatenate([high, low, high], axis=0)) + bias_ref[...]
+    for n, (x, t) in enumerate(tiles):
+        output_ref[x, :, t, :] = mixed[:, n * plan.nz : (n + 1) * plan.nz].reshape(plan.c, 8, plan.nz)
 
 
 def pick(plan, own_ref, mirror_ref, order_ref, chosen_ref, ordered_ref):
@@ -349,7 +369,7 @@
 
 
 def mix_kernel(
-    plan, own_ref, mirror_ref, order_ref, disorder_ref, chosen_ref, back_ref, weight_ref,
+    plan, after_ref, own_ref, mirror_ref, order_ref, disorder_ref, chosen_ref, back_ref, weight_ref,
     modes_ref, own_out, mirror_out, ordered_ref, made_ref, sums_ref,
 ):
     wk, quarters = plan.wk, 128 // plan.mx
@@ -372,7 +392,7 @@
 
 
 def mix_back_kernel(
-    plan, own_ref, mirror_ref, order_ref, disorder_ref, chosen_ref, back_ref, weight_ref, modes_ref,
+    plan, after_ref, own_ref, mirror_ref, order_ref, disorder_ref, chosen_ref, back_ref, weight_ref, modes_ref,
     gradient_ref, own_out, mirror_out, ordered_ref, made_ref, sums_ref,
 ):
     wk, quarters = plan.wk, 128 // plan.mx
@@ -421,6 +441,10 @@
     return jax.ShapeDtypeStruct(shape, f32)
 
 
+def anywhere():
+    return pl.BlockSpec(memory_space=pl.ANY)
+
+
 def scalar():
     return pl.BlockSpec(memory_space=pltpu.SMEM)
 
@@ -442,7 +466,7 @@
 class Program:
     def __init__(self, plan):
         self.plan = plan
-        self.plane = [jnp.asarray(t) for t in plan.plane_table()]
+        self.plane = jnp.asarray(plan.plane_table())
         self.depth = jnp.asarray(plan.depth_forward())
         self.inverse = jnp.asarray(plan.depth_inverse())
         slab, chan = lax.axis_index("slab"), lax.axis_index("chan")
@@ -469,9 +493,9 @@
         plan = self.plan
         return leading((plan.xb, plan.c, plan.ny, plan.nz))
 
-    def tables(self):
-        plan = self.plan
-        return [leading((plan.blk, 2 * plan.lp))] * 2
+    def table(self):
+        plan = self.plan
+        return leading((1, 3 * plan.blk, 2 * plan.lp))
 
     def lines(self):
         plan = self.plan
@@ -487,10 +511,10 @@
         half = self.half_shape()
         return call(
             partial(analyse_kernel, plan), "analyse", plan.nx // plan.xb,
-            [scalar(), self.field_spec(), *self.tables(), whole(self.depth), whole(self.turn)],
+            [scalar(), self.field_spec(), self.table(), whole(self.depth), whole(self.turn)],
             [whole_shape(half)] * 2, [shaped(*half)] * 2,
             [self.lines(), self.spectra()[0]], self.matmul, self.field,
-        )(self.flag, values, *self.plane, self.depth, self.turn)
+        )(self.flag, values, self.plane, self.depth, self.turn)
 
     def middle(self, own, other, linear, cotangent):
         plan = self.plan
@@ -498,41 +522,41 @@
         field = shaped(plan.nx, plan.c, plan.ny, plan.nz)
         return call(
             partial(middle_kernel, plan), "middle", plan.nx // plan.xb,
-            [scalar(), whole_shape(half), whole_shape(half), self.field_spec(), self.field_spec(), *self.tables(),
+            [scalar(), whole_shape(half), whole_shape(half), self.field_spec(), self.field_spec(), self.table(),
              whole(self.depth), whole(self.inverse), whole(self.turn)],
             [self.field_spec(), self.field_spec(), whole_shape(half), whole_shape(half)],
             [field, field, shaped(*half), shaped(*half)],
             [self.lines(), self.lines(), *self.spectra()], 2 * self.matmul, 4 * self.field,
-        )(self.flag, own, other, linear, cotangent, *self.plane, self.depth, self.inverse, self.turn)
+        )(self.flag, own, other, linear, cotangent, self.plane, self.depth, self.inverse, self.turn)
 
     def synthesise(self, own, other, linear):
         plan = self.plan
         half = self.half_shape()
         return call(
             partial(synthesise_kernel, plan), "synthesise", plan.nx // plan.xb,
-            [scalar(), whole_shape(half), whole_shape(half), self.field_spec(), *self.tables(),
+            [scalar(), whole_shape(half), whole_shape(half), self.field_spec(), self.table(),
              whole(self.inverse), whole(self.turn)],
             self.field_spec(), shaped(plan.nx, plan.c, plan.ny, plan.nz),
             [self.lines(), *self.spectra()], self.matmul, 2 * self.field,
-        )(self.flag, own, other, linear, *self.plane, self.inverse, self.turn)
-
-    def linear(self, values, matrix, bias):
+        )(self.flag, own, other, linear, self.plane, self.inverse, self.turn)
+
+    def linear(self, after, values, matrix, bias):
         plan = self.plan
         wide = jnp.kron(matrix, jnp.eye(8, dtype=f32))
         column = jnp.repeat(bias, 8)[:, None]
-        spec = leading((1, plan.c, plan.ny, plan.nz))
+        spec = leading((plan.lb, plan.c, plan.ny, plan.nz))
         return call(
-            partial(linear_kernel, plan), "linear", plan.nx,
-            [spec, whole(wide), whole(column)],
+            partial(linear_kernel, plan), "linear", plan.nx // plan.lb,
+            [anywhere(), spec, whole(wide), whole(column)],
             spec, shaped(plan.nx, plan.c, plan.ny, plan.nz), [],
             6 * (8 * plan.c) ** 2 * plan.nx * plan.ny // 8 * plan.nz, 2 * self.field,
-        )(values, wide, column)
+        )(after, values, wide, column)
 
     def mix_specs(self):
         plan = self.plan
         modes = (plan.rt, plan.ll)
         ins = [
-            whole_shape(modes), whole_shape(modes), whole(self.order), whole(self.disorder),
+            anywhere(), whole_shape(modes), whole_shape(modes), whole(self.order), whole(self.disorder),
             leading((1,) + self.chosen.shape[1:]), leading((1,) + self.back.shape[1:]),
             leading((1, 2, plan.c, plan.wk, plan.c * plan.mx)),
         ]
@@ -543,23 +567,23 @@
         ]
         return ins, [whole_shape(modes)] * 2, [shaped(*modes)] * 2, scratch
 
-    def mix(self, own, mirror, weights):
+    def mix(self, after, own, mirror, weights):
         plan = self.plan
         ins, outs, shapes, scratch = self.mix_specs()
         kept = leading((1, plan.rows, 256))
         return call(
             partial(mix_kernel, plan), "mix", plan.wb, ins, [kept, *outs],
             [shaped(plan.wb, plan.rows, 256), *shapes], scratch, 10**9, 4 * weights.size,
-        )(own, mirror, self.order, self.disorder, self.chosen, self.back, weights)
-
-    def mix_back(self, own, mirror, weights, modes):
+        )(after, own, mirror, self.order, self.disorder, self.chosen, self.back, weights)
+
+    def mix_back(self, after, own, mirror, weights, modes):
         plan = self.plan
         ins, outs, shapes, scratch = self.mix_specs()
         kept = leading((1, plan.rows, 256))
         return call(
             partial(mix_back_kernel, plan), "mix_back", plan.wb, ins + [kept], [ins[-1], *outs],
             [shaped(*weights.shape), *shapes], scratch, 10**9, 8 * weights.size,
-        )(own, mirror, self.order, self.disorder, self.chosen, self.back, weights, modes)
+        )(after, own, mirror, self.order, self.disorder, self.chosen, self.back, weights, modes)
 
     def across(self, value, axis, bit):
         size = lax.axis_size(axis)
@@ -622,14 +646,15 @@
     program = Program(plan)
     values = jnp.transpose(inputs, (0, 2, 1, 3))
     weights = jnp.transpose(spectral, (0, 2, 3, 1, 4))
-    own, mirror = program.gather_sums(*program.analyse(values))
-    linear = program.linear(values, local_weight.T, bias_vector)
-    modes, own, mirror = program.mix(own, mirror, weights)
+    keep, send = program.analyse(values)
+    linear = program.linear(send, values, local_weight.T, bias_vector)
+    own, mirror = program.gather_sums(keep, send)
+    modes, own, mirror = program.mix(linear, own, mirror, weights)
     own, other = program.spread_modes(own, mirror)
     output, gradient, keep, send = program.middle(own, other, linear, jnp.transpose(cotangent, (0, 2, 1, 3)))
+    linear = program.linear(send, gradient, local_weight, jnp.zeros_like(bias_vector))
     own, mirror = program.gather_sums(keep, send)
-    linear = program.linear(gradient, local_weight, jnp.zeros_like(bias_vector))
-    grad_spectral, own, mirror = program.mix_back(own, mirror, weights, modes)
+    grad_spectral, own, mirror = program.mix_back(linear, own, mirror, weights, modes)
     own, other = program.spread_modes(own, mirror)
     grad_inputs = program.synthesise(own, other, linear)
     return (

time: 522 us -> 438 us (0.84)
  Pallas kernels: 212 us -> 145 us
  starting transfers between devices: 45.1 us -> 35.1 us
  waiting for transfers between devices: 213 us -> 206 us
    pallas_call x2, Pallas kernels: 48.2 us -> 24.1 us  [linear(): call(partial(linear_kernel, plan), 'linear', plan.nx // plan.lb, [anywher...]
    ppermute x4, waiting for transfers between devices: 32.6 us -> 12.5 us  [mirrored(): lax.ppermute(value, ('slab', 'chan'), [(i, total - 1 - i) for i in range(...]
    pallas_call x1, Pallas kernels: 67.4 us -> 47.8 us  [middle(): call(partial(middle_kernel, plan), 'middle', plan.nx // plan.xb, [scalar(...]
    ppermute x20, starting transfers between devices: 41.9 us -> 26 us  [across(): return lax.ppermute(value, axis, [(i, i ^ bit) for i in range(size)])]
    ppermute x20, waiting for transfers between devices: 181 us -> 193 us  [across(): return lax.ppermute(value, axis, [(i, i ^ bit) for i in range(size)])]
    pallas_call x1, Pallas kernels: 30.3 us -> 19.5 us  [synthesise(): call(partial(synthesise_kernel, plan), 'synthesise', plan.nx // plan.xb,...]
    pallas_call x1, Pallas kernels: 36.9 us -> 27.2 us  [analyse(): call(partial(analyse_kernel, plan), 'analyse', plan.nx // plan.xb, [scala...]
    ppermute x4, starting transfers between devices: 3.18 us -> 9.12 us  [mirrored(): lax.ppermute(value, ('slab', 'chan'), [(i, total - 1 - i) for i in range(...]
  transfers between devices with their start and end apart: 24 -> 24, of which waited for: 18 -> 19; matrix products, arithmetic and copies ran while one was open for 5% -> 6% of each run, Pallas kernels for 9% -> 6%
where the time goes in v2:
time: 438 us; the launch traced here: 437 us
  waiting for transfers between devices  206 us (47%)
  Pallas kernels  145 us (33%)
  local copies, waits for them, and re-layouts  38.3 us (9%)
  starting transfers between devices  35.1 us (8%)
  other arithmetic  12 us (3%)
    ppermute x20, waiting for transfers between devices, across(): return lax.ppermute(value, axis, [(i, i ^ bit) for i in range(size)])  193 us
    pallas_call x1, Pallas kernels, middle(): call(partial(middle_kernel, plan), 'middle', plan.nx // plan.xb, [scalar(...  47.8 us
    pallas_call x1, Pallas kernels, analyse(): call(partial(analyse_kernel, plan), 'analyse', plan.nx // plan.xb, [scala...  27.2 us
    ppermute x20, starting transfers between devices, across(): return lax.ppermute(value, axis, [(i, i ^ bit) for i in range(size)])  26 us
    pallas_call x2, Pallas kernels, linear(): call(partial(linear_kernel, plan), 'linear', plan.nx // plan.lb, [anywher...  24.1 us
    unnamed x24, local copies, waits for them, and re-layouts  23.3 us
    pallas_call x1, Pallas kernels, synthesise(): call(partial(synthesise_kernel, plan), 'synthesise', plan.nx // plan.xb,...  19.5 us
    pallas_call x1, Pallas kernels, mix_back(): call(partial(mix_back_kernel, plan), 'mix_back', plan.wb, ins + [kept], [...  14 us
  transfers between devices with their start and end apart: 24, of which 19 were waited for; matrix products, arithmetic and copies ran while one was open for 6% of the time, Pallas kernels for 6%

profile of v2, /device:TPU:0, one launch (start us, length us, event | category | flops | bytes accessed | tf_op | source)
XLA Modules:
  0.0 436.8 jit_solution(1082026493379506288)
XLA Ops:
  1.9 27.2 %analyse.1 = (f32[2,2,184,640]{3,2,1,0:T(8,128)}, f32[2,2,184,640]{3,2,1,0:T(8,128)}) custom-call(s32[1]{0:T(128)} %bitcast.flag_ref, f32[32,20,32,128]{3,2,1,0:T(8,128)} %bitcast.147, bf16[4,768,1280]{2,1,0:T(8,128)(2,1)} %constant.146.clone.plane_ref, bf16[80,256]{1,0:T(8,128)(2,1)} %constant.147.clone.depth_ref, f32[2,640]{1,0:T(2,128)} %fusion.4.turn_ref), custom_call_target="tpu_custom_call" | custom-call | flops 6291456000 | bytes 10485760 | tf_op jit(solution)/shard_map/analyse/pallas_call | solution.py:512
  40.8 21.2 %collective-permute-done.1 = f32[1,2,184,640]{3,2,1,0:T(8,128)S(1)} collective-permute-done((f32[1,2,184,640]{3,2,1,0:T(8,128)}, f32[1,2,184,640]{3,2,1,0:T(8,128)S(1)}, u32[]{:S(2)}, u32[]{:S(2)}) %collective-permute-start.1) | collective-permute-done | bytes 942112 | tf_op jit(solution)/shard_map/ppermute | solution.py:590
  72.0 9.1 %collective-permute-done.4 = f32[184,384]{1,0:T(8,128)S(1)} collective-permute-done((f32[184,384]{1,0:T(8,128)S(1)}, f32[184,384]{1,0:T(8,128)S(1)}, u32[]{:S(2)}, u32[]{:S(2)}) %collective-permute-start.4) | collective-permute-done | bytes 282656 | tf_op jit(solution)/shard_map/ppermute | solution.py:590
  81.1 10.4 %collective-permute-done.3 = f32[184,384]{1,0:T(8,128)S(1)} collective-permute-done((f32[184,384]{1,0:T(8,128)S(1)}, f32[184,384]{1,0:T(8,128)S(1)}, u32[]{:S(2)}, u32[]{:S(2)}) %collective-permute-start.3) | collective-permute-done | bytes 282656 | tf_op jit(solution)/shard_map/ppermute | solution.py:590
  97.9 6.8 %copy.27 = f32[8,8,2,20,640]{4,1,3,2,0:T(8,128)} copy(f32[8,8,2,20,640]{4,2,3,1,0:T(2,128)} %param.14) | data formatting | bytes 13107200 | tf_op args[2]
  104.7 12.0 %linear.2.after_ref.linear_ref = f32[32,20,32,128]{3,2,1,0:T(8,128)} custom-call(f32[2,2,184,640]{3,2,1,0:T(8,128)} %get-tuple-element.15.after_ref, f32[32,20,32,128]{3,2,1,0:T(8,128)} %bitcast.148, f32[160,160]{1,0:T(8,128)} %mul.44.matrix_ref, f32[160,1]{1,0:T(8,128)} %broadcast_in_dim_reshape.8.bias_ref), custom_call_target="tpu_custom_call" | custom-call | flops 2516582400 | bytes 20971520 | tf_op jit(solution)/shard_map/linear/pallas_call | solution.py:548
  117.4 12.4 %mix.1 = (f32[8,160,256]{2,1,0:T(8,128)}, f32[184,384]{1,0:T(8,128)}, f32[184,384]{1,0:T(8,128)}) custom-call(f32[32,20,32,128]{3,2,1,0:T(8,128)} %linear.2.after_ref.linear_ref, f32[184,384]{1,0:T(8,128)} %copy-done.3, f32[184,384]{1,0:T(8,128)} %copy-done.5, bf16[160,184]{1,0:T(8,128)(2,1)} %copy.23.order_ref, ...), custom_call_target="tpu_custom_call" | custom-call | flops 1000000000 | bytes 6553600 | tf_op jit(solution)/shard_map/mix/pallas_call | solution.py:574
  133.0 6.3 %collective-permute-done.6 = f32[184,384]{1,0:T(8,128)S(1)} collective-permute-done((f32[184,384]{1,0:T(8,128)}, f32[184,384]{1,0:T(8,128)S(1)}, u32[]{:S(2)}, u32[]{:S(2)}) %collective-permute-start.6) | collective-permute-done | bytes 282656 | tf_op jit(solution)/shard_map/ppermute | solution.py:594
  145.6 4.8 %collective-permute-done.9 = f32[184,384]{1,0:T(8,128)S(1)} collective-permute-done((f32[184,384]{1,0:T(8,128)S(1)}, f32[184,384]{1,0:T(8,128)S(1)}, u32[]{:S(2)}, u32[]{:S(2)}) %collective-permute-start.9) | collective-permute-done | bytes 282656 | tf_op jit(solution)/shard_map/ppermute | solution.py:590
  150.5 19.5 %collective-permute-done.8 = f32[184,384]{1,0:T(8,128)S(1)} collective-permute-done((f32[184,384]{1,0:T(8,128)S(1)}, f32[184,384]{1,0:T(8,128)S(1)}, u32[]{:S(2)}, u32[]{:S(2)}) %collective-permute-start.8) | collective-permute-done | bytes 282656 | tf_op jit(solution)/shard_map/ppermute | solution.py:590
  175.5 22.7 %collective-permute-done.10 = f32[1,2,184,640]{3,2,1,0:T(8,128)} collective-permute-done((f32[1,2,184,640]{3,2,1,0:T(8,128)}, f32[1,2,184,640]{3,2,1,0:T(8,128)}, u32[]{:S(2)}, u32[]{:S(2)}) %collective-permute-start.10) | collective-permute-done | bytes 942112 | tf_op jit(solution)/shard_map/ppermute | solution.py:590
  206.0 47.8 %middle.1 = (f32[32,20,32,128]{3,2,1,0:T(8,128)}, f32[32,20,32,128]{3,2,1,0:T(8,128)}, f32[2,2,184,640]{3,2,1,0:T(8,128)}, f32[2,2,184,640]{3,2,1,0:T(8,128)}) custom-call(s32[1]{0:T(128)} %bitcast.flag_ref, f32[2,2,184,640]{3,2,1,0:T(8,128)} %copy-done.1, f32[2,2,184,640]{3,2,1,0:T(8,128)} %copy-done.10, f32[32,20,32,128]{3,2,1,0:T(8,128)} %linear.2.after_ref.linear_ref, ...), custom_call_target="tpu_custom_call" | custom-call | flops 12582912000 | bytes 41943040 | tf_op jit(solution)/shard_map/middle/pallas_call | solution.py:523
  260.4 22.4 %collective-permute-done.13 = f32[1,2,184,640]{3,2,1,0:T(8,128)S(1)} collective-permute-done((f32[1,2,184,640]{3,2,1,0:T(8,128)S(1)}, f32[1,2,184,640]{3,2,1,0:T(8,128)S(1)}, u32[]{:S(2)}, u32[]{:S(2)}) %collective-permute-start.13) | collective-permute-done | bytes 942112 | tf_op jit(solution)/shard_map/ppermute | solution.py:590
  287.3 7.1 %collective-permute-done.14 = f32[184,384]{1,0:T(8,128)S(1)} collective-permute-done((f32[184,384]{1,0:T(8,128)S(1)}, f32[184,384]{1,0:T(8,128)S(1)}, u32[]{:S(2)}, u32[]{:S(2)}) %collective-permute-start.14) | collective-permute-done | bytes 282656 | tf_op jit(solution)/shard_map/ppermute | solution.py:590
  294.4 5.6 %collective-permute-done.16 = f32[184,384]{1,0:T(8,128)S(1)} collective-permute-done((f32[184,384]{1,0:T(8,128)S(1)}, f32[184,384]{1,0:T(8,128)S(1)}, u32[]{:S(2)}, u32[]{:S(2)}) %collective-permute-start.16) | collective-permute-done | bytes 282656 | tf_op jit(solution)/shard_map/ppermute | solution.py:590
  300.0 11.2 %collective-permute-done.15 = f32[184,384]{1,0:T(8,128)S(1)} collective-permute-done((f32[184,384]{1,0:T(8,128)S(1)}, f32[184,384]{1,0:T(8,128)S(1)}, u32[]{:S(2)}, u32[]{:S(2)}) %collective-permute-start.15) | collective-permute-done | bytes 282656 | tf_op jit(solution)/shard_map/ppermute | solution.py:590
  314.3 12.0 %linear.3.after_ref.linear_ref = f32[32,20,32,128]{3,2,1,0:T(8,128)} custom-call(f32[2,2,184,640]{3,2,1,0:T(8,128)} %get-tuple-element.20.after_ref, f32[32,20,32,128]{3,2,1,0:T(8,128)} %get-tuple-element.21.values_ref, f32[160,160]{1,0:T(8,128)} %mul.47.matrix_ref, f32[160,1]{1,0:T(8,128)} %broadcast_in_dim_reshape.7.bias_ref), custom_call_target="tpu_custom_call" | custom-call | flops 2516582400 | bytes 20971520 | tf_op jit(solution)/shard_map/linear/pallas_call | solution.py:548
  327.1 14.0 %mix_back.1 = (f32[8,2,20,8,640]{4,3,2,1,0:T(8,128)}, f32[184,384]{1,0:T(8,128)}, f32[184,384]{1,0:T(8,128)}) custom-call(f32[32,20,32,128]{3,2,1,0:T(8,128)} %linear.3.after_ref.linear_ref, f32[184,384]{1,0:T(8,128)} %copy-done.4, f32[184,384]{1,0:T(8,128)} %copy-done.6, bf16[160,184]{1,0:T(8,128)(2,1)} %copy.23.order_ref, ...), custom_call_target="tpu_custom_call" | custom-call | flops 1000000000 | bytes 13107200 | tf_op jit(solution)/shard_map/mix_back/pallas_call | solution.py:583
  344.4 6.2 %collective-permute-done.18 = f32[184,384]{1,0:T(8,128)S(1)} collective-permute-done((f32[184,384]{1,0:T(8,128)}, f32[184,384]{1,0:T(8,128)S(1)}, u32[]{:S(2)}, u32[]{:S(2)}) %collective-permute-start.18) | collective-permute-done | bytes 282656 | tf_op jit(solution)/shard_map/ppermute | solution.py:594
  353.4 5.6 %collective-permute-start.20 = (f32[184,384]{1,0:T(8,128)S(1)}, f32[184,384]{1,0:T(8,128)S(1)}, u32[]{:S(2)}, u32[]{:S(2)}) collective-permute-start(f32[184,384]{1,0:T(8,128)S(1)} %add.117), channel_id=1, source_target_pairs={{0,8},{4,12},{8,0},{12,4},{1,9},{5,13},{9,1},{13,5},{2,10},{6,14},... | collective-permute-start | bytes 847880 | tf_op jit(solution)/shard_map/ppermute | solution.py:590
  361.7 19.6 %collective-permute-done.20 = f32[184,384]{1,0:T(8,128)S(1)} collective-permute-done((f32[184,384]{1,0:T(8,128)S(1)}, f32[184,384]{1,0:T(8,128)S(1)}, u32[]{:S(2)}, u32[]{:S(2)}) %collective-permute-start.20) | collective-permute-done | bytes 282656 | tf_op jit(solution)/shard_map/ppermute | solution.py:590
  383.1 22.4 %collective-permute-done.22 = f32[1,2,184,640]{3,2,1,0:T(8,128)S(1)} collective-permute-done((f32[1,2,184,640]{3,2,1,0:T(8,128)S(1)}, f32[1,2,184,640]{3,2,1,0:T(8,128)S(1)}, u32[]{:S(2)}, u32[]{:S(2)}) %collective-permute-start.22) | collective-permute-done | bytes 942112 | tf_op jit(solution)/shard_map/ppermute | solution.py:590
  405.9 11.3 %copy.25 = f32[8,8,2,20,640]{4,2,3,1,0:T(2,128)} copy(f32[8,8,2,20,640]{4,1,3,2,0:T(8,128)} %bitcast.150) | data formatting | bytes 13107200
  417.2 19.5 %synthesise.1 = f32[32,20,32,128]{3,2,1,0:T(8,128)} custom-call(s32[1]{0:T(128)} %bitcast.flag_ref, f32[2,2,184,640]{3,2,1,0:T(8,128)} %copy-done, f32[2,2,184,640]{3,2,1,0:T(8,128)} %collective-permute-done.23.other_ref, f32[32,20,32,128]{3,2,1,0:T(8,128)} %linear.3.after_ref.linear_ref, bf16[4,768,1280]{2,1,0:T(8,128)(2,1)} %constant.146.clone.plane_ref, ...), custom_call_target="tpu_custom_call" | custom-call | flops 6291456000 | bytes 20971520 | tf_op jit(solution)/shard_map/synthesise/pallas_call | solution.py:535
  (107 shorter events, 78.9 us)
Async XLA Ops:
  29.1 4.2 collective-permute-start
  37.8 24.2 %collective-permute-start.1 = (f32[1,2,184,640]{3,2,1,0:T(8,128)}, f32[1,2,184,640]{3,2,1,0:T(8,128)S(1)}, u32[]{:S(2)}, u32[]{:S(2)}) collective-permute-start(f32[1,2,184,640]{3,2,1,0:T(8,128)} %constant_dynamic-slice_fusion.1), channel_id=1, source_target_pairs={{0,2},{1,3},{2,0},{3,1},{4,6},{5,7},{6,4},{7,5},{8,10},{9,11},{10,... | collective-permute-start | bytes 2826248 | tf_op jit(solution)/shard_map/ppermute | solution.py:590
  62.9 9.1 %collective-permute-start.2 = (f32[184,384]{1,0:T(8,128)S(1)}, f32[184,384]{1,0:T(8,128)S(1)}, u32[]{:S(2)}, u32[]{:S(2)}) collective-permute-start(f32[184,384]{1,0:T(8,128)S(1)} %get-tuple-element.48), channel_id=1, source_target_pairs={{0,4},{4,0},{8,12},{12,8},{1,5},{5,1},{9,13},{13,9},{2,6},{6,2},{1... | collective-permute-start | bytes 847880 | tf_op jit(solution)/shard_map/ppermute | solution.py:590
  64.8 16.3 %collective-permute-start.4 = (f32[184,384]{1,0:T(8,128)S(1)}, f32[184,384]{1,0:T(8,128)S(1)}, u32[]{:S(2)}, u32[]{:S(2)}) collective-permute-start(f32[184,384]{1,0:T(8,128)S(1)} %get-tuple-element.49), channel_id=1, source_target_pairs={{0,12},{4,8},{8,4},{12,0},{1,13},{5,9},{9,5},{13,1},{2,14},{6,10},... | collective-permute-start | bytes 847880 | tf_op jit(solution)/shard_map/ppermute | solution.py:590
  67.3 24.2 %collective-permute-start.3 = (f32[184,384]{1,0:T(8,128)S(1)}, f32[184,384]{1,0:T(8,128)S(1)}, u32[]{:S(2)}, u32[]{:S(2)}) collective-permute-start(f32[184,384]{1,0:T(8,128)S(1)} %get-tuple-element.50), channel_id=1, source_target_pairs={{0,8},{4,12},{8,0},{12,4},{1,9},{5,13},{9,1},{13,5},{2,10},{6,14},... | collective-permute-start | bytes 847880 | tf_op jit(solution)/shard_map/ppermute | solution.py:590
  91.6 25.1 %collective-permute-start.5 = (f32[184,384]{1,0:T(8,128)S(1)}, f32[184,384]{1,0:T(8,128)S(1)}, u32[]{:S(2)}, u32[]{:S(2)}) collective-permute-start(f32[184,384]{1,0:T(8,128)S(1)} %fusion.3.own_ref), channel_id=1, source_target_pairs={{0,15},{1,14},{2,13},{3,12},{4,11},{5,10},{6,9},{7,8},{8,7},{9,6},... | collective-permute-start | bytes 847880 | tf_op jit(solution)/shard_map/ppermute | solution.py:594
  129.8 9.5 %collective-permute-start.6 = (f32[184,384]{1,0:T(8,128)}, f32[184,384]{1,0:T(8,128)S(1)}, u32[]{:S(2)}, u32[]{:S(2)}) collective-permute-start(f32[184,384]{1,0:T(8,128)} %get-tuple-element.18), channel_id=1, source_target_pairs={{0,15},{1,14},{2,13},{3,12},{4,11},{5,10},{6,9},{7,8},{8,7},{9,6},... | collective-permute-start | bytes 847880 | tf_op jit(solution)/shard_map/ppermute | solution.py:594
  140.3 10.2 %collective-permute-start.9 = (f32[184,384]{1,0:T(8,128)S(1)}, f32[184,384]{1,0:T(8,128)S(1)}, u32[]{:S(2)}, u32[]{:S(2)}) collective-permute-start(f32[184,384]{1,0:T(8,128)S(1)} %add.111), channel_id=1, source_target_pairs={{0,12},{4,8},{8,4},{12,0},{1,13},{5,9},{9,5},{13,1},{2,14},{6,10},... | collective-permute-start | bytes 847880 | tf_op jit(solution)/shard_map/ppermute | solution.py:590
  142.1 27.8 %collective-permute-start.8 = (f32[184,384]{1,0:T(8,128)S(1)}, f32[184,384]{1,0:T(8,128)S(1)}, u32[]{:S(2)}, u32[]{:S(2)}) collective-permute-start(f32[184,384]{1,0:T(8,128)S(1)} %add.111), channel_id=1, source_target_pairs={{0,8},{4,12},{8,0},{12,4},{1,9},{5,13},{9,1},{13,5},{2,10},{6,14},... | collective-permute-start | bytes 847880 | tf_op jit(solution)/shard_map/ppermute | solution.py:590
  145.6 24.3 %collective-permute-start.7 = (f32[184,384]{1,0:T(8,128)S(1)}, f32[184,384]{1,0:T(8,128)S(1)}, u32[]{:S(2)}, u32[]{:S(2)}) collective-permute-start(f32[184,384]{1,0:T(8,128)S(1)} %add.111), channel_id=1, source_target_pairs={{0,4},{4,0},{8,12},{12,8},{1,5},{5,1},{9,13},{13,9},{2,6},{6,2},{1... | collective-permute-start | bytes 847880 | tf_op jit(solution)/shard_map/ppermute | solution.py:590
  174.9 23.2 %collective-permute-start.10 = (f32[1,2,184,640]{3,2,1,0:T(8,128)}, f32[1,2,184,640]{3,2,1,0:T(8,128)}, u32[]{:S(2)}, u32[]{:S(2)}) collective-permute-start(f32[1,2,184,640]{3,2,1,0:T(8,128)} %maximum_bitcast_fusion.2), channel_id=1, source_target_pairs={{0,2},{1,3},{2,0},{3,1},{4,6},{5,7},{6,4},{7,5},{8,10},{9,11},{10,... | collective-permute-start | bytes 2826248 | tf_op jit(solution)/shard_map/ppermute | solution.py:590
  200.9 3.9 collective-permute-start.11
  253.8 4.1 collective-permute-start.12
  259.8 23.0 %collective-permute-start.13 = (f32[1,2,184,640]{3,2,1,0:T(8,128)S(1)}, f32[1,2,184,640]{3,2,1,0:T(8,128)S(1)}, u32[]{:S(2)}, u32[]{:S(2)}) collective-permute-start(f32[1,2,184,640]{3,2,1,0:T(8,128)S(1)} %constant_dynamic-slice_fusion), channel_id=1, source_target_pairs={{0,2},{1,3},{2,0},{3,1},{4,6},{5,7},{6,4},{7,5},{8,10},{9,11},{10,... | collective-permute-start | bytes 2826248 | tf_op jit(solution)/shard_map/ppermute | solution.py:590
  283.8 10.6 %collective-permute-start.14 = (f32[184,384]{1,0:T(8,128)S(1)}, f32[184,384]{1,0:T(8,128)S(1)}, u32[]{:S(2)}, u32[]{:S(2)}) collective-permute-start(f32[184,384]{1,0:T(8,128)S(1)} %get-tuple-element.41), channel_id=1, source_target_pairs={{0,4},{4,0},{8,12},{12,8},{1,5},{5,1},{9,13},{13,9},{2,6},{6,2},{1... | collective-permute-start | bytes 847880 | tf_op jit(solution)/shard_map/ppermute | solution.py:590
  283.8 16.1 %collective-permute-start.16 = (f32[184,384]{1,0:T(8,128)S(1)}, f32[184,384]{1,0:T(8,128)S(1)}, u32[]{:S(2)}, u32[]{:S(2)}) collective-permute-start(f32[184,384]{1,0:T(8,128)S(1)} %get-tuple-element.42), channel_id=1, source_target_pairs={{0,12},{4,8},{8,4},{12,0},{1,13},{5,9},{9,5},{13,1},{2,14},{6,10},... | collective-permute-start | bytes 847880 | tf_op jit(solution)/shard_map/ppermute | solution.py:590
  286.3 24.9 %collective-permute-start.15 = (f32[184,384]{1,0:T(8,128)S(1)}, f32[184,384]{1,0:T(8,128)S(1)}, u32[]{:S(2)}, u32[]{:S(2)}) collective-permute-start(f32[184,384]{1,0:T(8,128)S(1)} %get-tuple-element.43), channel_id=1, source_target_pairs={{0,8},{4,12},{8,0},{12,4},{1,9},{5,13},{9,1},{13,5},{2,10},{6,14},... | collective-permute-start | bytes 847880 | tf_op jit(solution)/shard_map/ppermute | solution.py:590
  311.3 15.1 %collective-permute-start.17 = (f32[184,384]{1,0:T(8,128)S(1)}, f32[184,384]{1,0:T(8,128)S(1)}, u32[]{:S(2)}, u32[]{:S(2)}) collective-permute-start(f32[184,384]{1,0:T(8,128)S(1)} %fusion.1.own_ref), channel_id=1, source_target_pairs={{0,15},{1,14},{2,13},{3,12},{4,11},{5,10},{6,9},{7,8},{8,7},{9,6},... | collective-permute-start | bytes 847880 | tf_op jit(solution)/shard_map/ppermute | solution.py:594
  341.1 9.5 %collective-permute-start.18 = (f32[184,384]{1,0:T(8,128)}, f32[184,384]{1,0:T(8,128)S(1)}, u32[]{:S(2)}, u32[]{:S(2)}) collective-permute-start(f32[184,384]{1,0:T(8,128)} %get-tuple-element.25), channel_id=1, source_target_pairs={{0,15},{1,14},{2,13},{3,12},{4,11},{5,10},{6,9},{7,8},{8,7},{9,6},... | collective-permute-start | bytes 847880 | tf_op jit(solution)/shard_map/ppermute | solution.py:594
  351.6 10.1 %collective-permute-start.21 = (f32[184,384]{1,0:T(8,128)S(1)}, f32[184,384]{1,0:T(8,128)S(1)}, u32[]{:S(2)}, u32[]{:S(2)}) collective-permute-start(f32[184,384]{1,0:T(8,128)S(1)} %add.117), channel_id=1, source_target_pairs={{0,12},{4,8},{8,4},{12,0},{1,13},{5,9},{9,5},{13,1},{2,14},{6,10},... | collective-permute-start | bytes 847880 | tf_op jit(solution)/shard_map/ppermute | solution.py:590
  353.4 27.8 %collective-permute-start.20 = (f32[184,384]{1,0:T(8,128)S(1)}, f32[184,384]{1,0:T(8,128)S(1)}, u32[]{:S(2)}, u32[]{:S(2)}) collective-permute-start(f32[184,384]{1,0:T(8,128)S(1)} %add.117), channel_id=1, source_target_pairs={{0,8},{4,12},{8,0},{12,4},{1,9},{5,13},{9,1},{13,5},{2,10},{6,14},... | collective-permute-start | bytes 847880 | tf_op jit(solution)/shard_map/ppermute | solution.py:590
  359.0 22.2 %collective-permute-start.19 = (f32[184,384]{1,0:T(8,128)S(1)}, f32[184,384]{1,0:T(8,128)S(1)}, u32[]{:S(2)}, u32[]{:S(2)}) collective-permute-start(f32[184,384]{1,0:T(8,128)S(1)} %add.117), channel_id=1, source_target_pairs={{0,4},{4,0},{8,12},{12,8},{1,5},{5,1},{9,13},{13,9},{2,6},{6,2},{1... | collective-permute-start | bytes 847880 | tf_op jit(solution)/shard_map/ppermute | solution.py:590
  382.6 22.9 %collective-permute-start.22 = (f32[1,2,184,640]{3,2,1,0:T(8,128)S(1)}, f32[1,2,184,640]{3,2,1,0:T(8,128)S(1)}, u32[]{:S(2)}, u32[]{:S(2)}) collective-permute-start(f32[1,2,184,640]{3,2,1,0:T(8,128)S(1)} %maximum_bitcast_fusion.3), channel_id=1, source_target_pairs={{0,2},{1,3},{2,0},{3,1},{4,6},{5,7},{6,4},{7,5},{8,10},{9,11},{10,... | collective-permute-start | bytes 2826248 | tf_op jit(solution)/shard_map/ppermute | solution.py:590
  405.8 11.4 %collective-permute-start.23 = (f32[2,2,184,640]{3,2,1,0:T(8,128)S(1)}, f32[2,2,184,640]{3,2,1,0:T(8,128)}, u32[]{:S(2)}, u32[]{:S(2)}) collective-permute-start(f32[2,2,184,640]{3,2,1,0:T(8,128)S(1)} %maximum_bitcast_fusion.1.own_ref), channel_id=1, source_target_pairs={{0,1},{1,0},{2,3},{3,2},{4,5},{5,4},{6,7},{7,6},{8,9},{9,8},{10,11... | collective-permute-start | bytes 5652488 | tf_op jit(solution)/shard_map/ppermute | solution.py:590
  (11 other events, 100.7 us)
